TPU v7x, 32 devices: a whole 2x2x4 slice. The times are simulated.
32 devices in a mesh: pipe: 2 (over y), dp: 4 (over z), tensor: 4 (over x, core).
Axes of the slice: x: 2, y: 2, z: 4, core: 2. Of those that a mesh axis runs over, the one named last changes fastest.
Arguments:
- acts_in: bfloat16 [8, 1024, 1024], P('dp', 'tensor'), may hold values from -6 to 6
- out_grad: bfloat16 [8, 1024, 1024], P('dp', 'tensor'), may hold values from -6 to 6
- mix_gain: bfloat16 [2, 1024], P('pipe', 'dp'), may hold values from 0.5 to 1.5
- w_mixer_in: bfloat16 [2, 1024, 2, 1536], P('pipe', 'dp', None, 'tensor'), may hold values from -0.1875 to 0.1875
- w_query: bfloat16 [2, 1024, 512], P('pipe', 'dp', 'tensor'), may hold values from -0.1875 to 0.1875
- w_shared: bfloat16 [2, 1024, 512], P('pipe', 'dp'), may hold values from -0.1875 to 0.1875
- w_step: bfloat16 [2, 1024, 24], P('pipe', 'dp'), may hold values from -0.1875 to 0.1875
- a_log: float32 [2, 24], P('pipe', 'tensor'), may hold values from 0 to 2.77
- dt_bias: float32 [2, 24], P('pipe', 'tensor'), may hold values from -7 to -2.3
- d_skip: float32 [2, 24], P('pipe', 'tensor'), may hold values from 0.5 to 1.5
- w_mamba_out: bfloat16 [2, 1536, 1024], P('pipe', 'tensor', 'dp'), may hold values from -0.3125 to 0.3125
- w_attn_out: bfloat16 [2, 512, 1024], P('pipe', 'tensor', 'dp'), may hold values from -1.5 to 1.5
- ffn_gain: bfloat16 [2, 1024], P('pipe', 'dp'), may hold values from 0.5 to 1.5
- w_gate_up: bfloat16 [2, 1024, 2, 2048], P('pipe', 'dp', None, 'tensor'), may hold values from -0.1875 to 0.1875
- w_down: bfloat16 [2, 2048, 1024], P('pipe', 'tensor', 'dp'), may hold values from -0.25 to 0.25
Outputs:
- acts_out: bfloat16 [2, 8, 1024, 1024], P('pipe', 'dp', 'tensor')
- in_grads: bfloat16 [2, 8, 1024, 1024], P('pipe', 'dp', 'tensor')
- grad_gains: float32 [2, 2, 1024], P('pipe', None, ('dp', 'tensor'))
- grad_mixer_in: float32 [2, 1024, 2, 1536], P('pipe', 'dp', None, 'tensor')
- grad_query: float32 [2, 1024, 512], P('pipe', 'dp', 'tensor')
- grad_shared: float32 [2, 1024, 512], P('pipe', ('dp', 'tensor'))
- grad_step: float32 [2, 1024, 24], P('pipe', ('dp', 'tensor'))
- grad_heads: float32 [2, 3, 24], P('pipe', None, 'tensor')
- grad_mamba_out: float32 [2, 1536, 1024], P('pipe', 'tensor', 'dp')
- grad_attn_out: float32 [2, 512, 1024], P('pipe', 'tensor', 'dp')
- grad_gate_up: float32 [2, 1024, 2, 2048], P('pipe', 'dp', None, 'tensor')
- grad_down: float32 [2, 2048, 1024], P('pipe', 'tensor', 'dp')
All inputs are finite; a program needn't handle non-finite values.
Results may differ from a plain program's by a relative error of at most 0.04.
Values may be sent and summed in bfloat16 or wider, within the bound.
A program may use at most 256 MiB of HBM per device.

v0:
```python
import functools

import jax
import jax.numpy as jnp
from jax import lax
from jax.experimental import pallas as pl
from jax.experimental.pallas import tpu as pltpu
from jax.sharding import PartitionSpec as P

HM = 24
HA = 8
KVH = 2
NS = 128
HD = 64
LANES = 128
STEP = 128
TILE = 256
EPS = 1e-05
F32 = jnp.float32
B16 = jnp.bfloat16
VMEM_LIMIT = 60 << 20
HEADS_AT = 32
GAINS_AT = 64


def nn(a, b):
    return lax.dot_general(a, b, (((1,), (0,)), ((), ())), preferred_element_type=F32)


def nt(a, b):
    return lax.dot_general(a, b, (((1,), (1,)), ((), ())), preferred_element_type=F32)


def tn(a, b):
    return lax.dot_general(a, b, (((0,), (0,)), ((), ())), preferred_element_type=F32)


def exact(a, b):
    return lax.dot_general(
        a, b, (((1,), (0,)), ((), ())), precision=lax.Precision.HIGHEST, preferred_element_type=F32
    )


def softplus(v):
    small = jnp.exp(-jnp.abs(v))
    series = small * (1.0 - small * (0.5 - small * (1.0 / 3.0 - small * 0.25)))
    return jnp.maximum(v, 0.0) + jnp.where(small < 0.02, series, jnp.log(1.0 + small))


def sigmoid(v):
    return 1.0 / (1.0 + jnp.exp(-v))


def iotas(rows, columns):
    return (
        lax.broadcasted_iota(jnp.int32, (rows, columns), 0),
        lax.broadcasted_iota(jnp.int32, (rows, columns), 1),
    )


def spread(column_block, head, rows):
    return jnp.broadcast_to(column_block[:, head : head + 1], (rows, LANES))


class Cols:
    def __init__(self, width):
        self.width = width
        self.z = 0
        self.u = width
        self.q = 2 * width
        self.b = self.q + LANES
        self.c = self.b + LANES
        self.k = self.c + LANES
        self.v = self.k + LANES
        self.step = self.v + LANES
        self.total = self.step + LANES
        self.pairs = width // LANES


class MixerRows:
    def __init__(self, cols, members):
        self.shared = 4 * LANES // members
        self.query = self.shared
        self.inner = self.query + LANES
        self.low = self.inner + 2 * cols.width
        self.total = self.low + cols.width + LANES


def fold_lanes(block):
    def folded(piece):
        count = piece // LANES
        size = block.shape[0] // count
        return jnp.concatenate([block[i * size : (i + 1) * size] for i in range(count)], axis=1)

    return folded


def unfold_lanes(block):
    return jnp.concatenate(
        [block[:, at : at + LANES] for at in range(0, block.shape[1], LANES)], axis=0
    )


def join_shared(cols, members, layer, q_heads, r):
    mixer, shared, few, rest = r.mixer, r.shared_w, r.few, r.rest
    ways, _, piece = mixer.shape
    at = MixerRows(cols, members)
    group = lax.axis_index(TENSOR) * q_heads // (HA // KVH)
    source, target = iotas(LANES, LANES)
    choose = (source == group * HD + (target & (HD - 1))).astype(B16)
    size = piece // members
    for d in range(ways):
        rows = slice(d * piece, (d + 1) * piece)
        rest[rows, :LANES] = unfold_lanes(mixer[d, at.query : at.query + LANES, :])
        for m in range(members):
            block = unfold_lanes(shared[m, d])
            to = slice(d * piece + m * size, d * piece + (m + 1) * size)
            for j in range(4):
                lanes = block[j * size : (j + 1) * size, :]
                if j >= 2:
                    lanes = nn(lanes, choose).astype(B16)
                rest[to, LANES * (j + 1) : LANES * (j + 2)] = lanes
        steps = few[layer, d, 8:16, :]
        steps = jnp.concatenate([steps, jnp.zeros((LANES - 8, piece), F32)], axis=0).T
        rest[rows, 5 * LANES :] = steps.astype(B16)


def split_heads(block, low_lanes):
    zero = jnp.zeros_like(block)
    return jnp.concatenate(
        [jnp.where(low_lanes, block, zero), jnp.where(low_lanes, zero, block)], axis=0
    )


def blocks_nn(rows_ref, rows, weights_ref, c, first=0):
    ways, _, piece = weights_ref.shape
    at = slice(first + c * piece, first + (c + 1) * piece)
    total = nn(rows_ref[rows, 0:piece], weights_ref[0, at, :])
    for d in range(1, ways):
        total += nn(rows_ref[rows, d * piece : (d + 1) * piece], weights_ref[d, at, :])
    return total


def multiply_out(lows_ref, weights_ref, first, part_ref, at=0):
    ways, _, piece = weights_ref.shape
    last = first + lows_ref.shape[1]

    def out_rows(i, _):
        rows = pl.ds(pl.multiple_of(i * TILE, TILE), TILE)
        block = lows_ref[rows, :]
        for k in range(ways):
            part_ref[rows, at + k * piece : at + (k + 1) * piece] = nn(
                block, weights_ref[k, first:last, :]
            ).astype(B16)
        return 0

    lax.fori_loop(0, lows_ref.shape[0] // TILE, out_rows, 0)


def multiply_back(grad_ref, weights_ref, first, count, part_ref, rows_ref, gain_sum, rest=None):
    ways, _, piece = weights_ref.shape
    gain_sum[...] = jnp.zeros_like(gain_sum)

    def out_rows(i, _):
        rows = pl.ds(pl.multiple_of(i * TILE, TILE), TILE)
        for d in range(ways):
            to = slice(d * piece, (d + 1) * piece)
            total = nt(grad_ref[rows, 0:piece], weights_ref[d, first : first + piece, :])
            for c in range(1, count):
                at = slice(first + c * piece, first + (c + 1) * piece)
                total += nt(grad_ref[rows, c * piece : (c + 1) * piece], weights_ref[d, at, :])
            if rest is not None:
                total += nt(grad_ref[rows, count * piece :], rest[to, :])
            part_ref[rows, to] = total.astype(B16)
            gain_sum[0:1, to] += jnp.sum(
                total * rows_ref[rows, to].astype(F32), axis=0, keepdims=True
            )
        return 0

    lax.fori_loop(0, grad_ref.shape[0] // TILE, out_rows, 0)


def skip_lanes(few_ref, layer, width):
    row, lane = iotas(width, LANES)
    own = ((row >> 6) == lane).astype(F32)
    skip = jnp.broadcast_to(few_ref[layer, 0, 4:5, :LANES], (8, LANES))
    return lax.dot_general(
        skip, own, (((1,), (1,)), ((), ())),
        precision=lax.Precision.HIGHEST, preferred_element_type=F32,
    )[0:1, :]


def core_fwd_phases(cols, members, layer, q_heads, r):
    rows_ref, weights_ref, few_ref = r.rows_mix, r.mixer, r.few
    proj_ref, step_ref, y_ref, lows_ref = r.proj, r.step, r.y, r.lows
    states_ref, lse_ref, part_ref, state = r.states, r.lse, r.part, r.state
    length = rows_ref.shape[0]
    width = cols.width
    piece = weights_ref.shape[2]

    at_row = MixerRows(cols, members)

    def join_all():
        join_shared(cols, members, layer, q_heads, r)

    def project_all():
        def project(i, _):
            rows = pl.ds(pl.multiple_of(i * TILE, TILE), TILE)
            for c in range(cols.q // piece):
                value = blocks_nn(rows_ref, rows, weights_ref, c, at_row.inner)
                proj_ref[rows, c * piece : (c + 1) * piece] = value.astype(B16)
            rest = nn(rows_ref[rows, :], r.rest[...])
            proj_ref[rows, cols.q : cols.b] = (rest[:, :LANES] * HD**-0.5).astype(B16)
            proj_ref[rows, cols.b : cols.step] = rest[:, LANES : 5 * LANES].astype(B16)
            step_ref[rows, :] = rest[:, 5 * LANES :]
            return 0

        lax.fori_loop(0, length // TILE, project, 0)

    def scan_all():
        ri, ci = iotas(STEP, STEP)
        lower = ri >= ci
        tril = lower.astype(F32)
        low_lanes = ci < HD
        decay = jnp.exp(few_ref[layer, 0, 2:3, :LANES])
        bias = few_ref[layer, 0, 3:4, :LANES]
        skips = skip_lanes(few_ref, layer, width)
        state[...] = jnp.zeros_like(state)

        def scan_block(b, _):
            rows = pl.ds(pl.multiple_of(b * STEP, STEP), STEP)
            dt = softplus(step_ref[rows, :] + bias)
            run = exact(tril, -dt * decay)
            run_t = run.T
            bm = proj_ref[rows, cols.b : cols.b + LANES]
            cm = proj_ref[rows, cols.c : cols.c + LANES]
            cb = jnp.where(lower, nt(cm, bm), 0.0)
            states_in = state[...]
            low_state = states_in.astype(B16)
            states_ref[b] = low_state
            carried = nn(cm, low_state)
            tails, fades = [], []
            for p in range(cols.pairs):
                lanes = slice(LANES * p, LANES * (p + 1))
                u = proj_ref[rows, cols.u + LANES * p : cols.u + LANES * (p + 1)].astype(F32)
                z = proj_ref[rows, cols.z + LANES * p : cols.z + LANES * (p + 1)].astype(F32)
                run_b = [spread(run, 2 * p + k, STEP) for k in range(2)]
                run_w = jnp.where(low_lanes, run_b[0], run_b[1])
                ud = u * jnp.where(low_lanes, spread(dt, 2 * p, STEP), spread(dt, 2 * p + 1, STEP))
                mix = jnp.concatenate(
                    [
                        (
                            jnp.exp(jnp.minimum(run_b[k] - run_t[2 * p + k : 2 * p + k + 1, :], 0.0))
                            * cb
                        ).astype(B16)
                        for k in range(2)
                    ],
                    axis=1,
                )
                inside = nn(mix, split_heads(ud, low_lanes).astype(B16))
                y = inside + carried[:, lanes] * jnp.exp(run_w) + skips[:, lanes] * u
                y_ref[rows, lanes] = y.astype(B16)
                lows_ref[rows, lanes] = (y * z * sigmoid(z)).astype(B16)
                end = run_w[STEP - 1 : STEP, :]
                tails.append((ud * jnp.exp(end - run_w)).astype(B16))
                fades.append(jnp.exp(end))
            fresh = tn(bm, jnp.concatenate(tails, axis=1))
            state[...] = states_in * jnp.concatenate(fades, axis=1) + fresh
            return 0

        lax.fori_loop(0, length // STEP, scan_block, 0)

    def attend_all():
        rk, ck = iotas(TILE, 2 * TILE)
        diagonal = rk <= jnp.where(ck < TILE, ck, ck - TILE)
        q_low = iotas(TILE, LANES)[1] < HD

        def attend(i, _):
            rows = pl.ds(pl.multiple_of(i * TILE, TILE), TILE)
            q2 = split_heads(proj_ref[rows, cols.q : cols.q + LANES], q_low)

            def piece(j, carry, masked):
                top, total, out = carry
                keys = pl.ds(pl.multiple_of(j * TILE, TILE), TILE)
                s = nt(proj_ref[keys, cols.k : cols.k + LANES], q2)
                if masked:
                    s = jnp.where(diagonal, s, -1e30)
                new_top = jnp.maximum(top, jnp.max(s, axis=0, keepdims=True))
                p = jnp.exp(s - new_top)
                scale = jnp.exp(top - new_top)
                total = total * scale + jnp.sum(p, axis=0, keepdims=True)
                out = out * scale + tn(proj_ref[keys, cols.v : cols.v + LANES], p.astype(B16))
                return new_top, total, out

            carry = (
                jnp.full((1, 2 * TILE), -1e30, F32),
                jnp.zeros((1, 2 * TILE), F32),
                jnp.zeros((LANES, 2 * TILE), F32),
            )
            carry = lax.fori_loop(0, i, lambda j, c: piece(j, c, False), carry)
            top, total, out = piece(i, carry, True)
            out = out / total
            joined = jnp.concatenate([out[:HD, :TILE], out[HD:, TILE:]], axis=0)
            lows_ref[rows, width : width + LANES] = joined.T.astype(B16)
            lse_ref[i] = jnp.broadcast_to(top + jnp.log(total), (8, 2 * TILE))
            return 0

        lax.fori_loop(0, length // TILE, attend, 0)

    def finish():
        multiply_out(lows_ref, weights_ref, at_row.low, part_ref)

    return [join_all, project_all, scan_all, attend_all, finish]


def core_bwd_phases(cols, layer, members, q_heads, r):
    back_ref, weights_ref, few_ref, rows_ref = r.rows_back, r.mixer, r.few, r.rows_mix
    proj_ref, step_ref, y_ref, lows_ref = r.proj, r.step, r.y, r.lows
    states_ref, lse_ref, part_ref = r.states, r.lse, r.part
    dproj_ref, heads_ref, dcore, grad_state, skip_sum = r.dproj, r.heads, r.dcore, r.grad_state, r.skip_sum
    dk_sum, dv_sum, folded, gain_sum, staged = r.dk_sum, r.dv_sum, r.folded, r.gain_sum, r.staged
    length = back_ref.shape[0]
    width = cols.width
    ways, _, piece = weights_ref.shape
    blocks = length // STEP
    depth = ways * piece
    at_row = MixerRows(cols, members)
    low_rows = slice(at_row.low, at_row.low + width + LANES)

    def into_all():
        def into_core(i, _):
            rows = pl.ds(pl.multiple_of(i * TILE, TILE), TILE)
            total = nt(back_ref[rows, 0:piece], weights_ref[0, low_rows, :])
            for k in range(1, ways):
                total += nt(
                    back_ref[rows, k * piece : (k + 1) * piece], weights_ref[k, low_rows, :]
                )
            dcore[rows, :] = total.astype(B16)
            return 0

        lax.fori_loop(0, length // TILE, into_core, 0)

    def attend_all():
        rk, ck = iotas(TILE, 2 * TILE)
        diagonal = rk <= jnp.where(ck < TILE, ck, ck - TILE)
        q_low = iotas(TILE, LANES)[1] < HD
        dk_sum[...] = jnp.zeros_like(dk_sum)
        dv_sum[...] = jnp.zeros_like(dv_sum)
        half = iotas(8, LANES)
        pick_low = (half[1] < HD).astype(F32)
        pick_high = (half[1] >= HD).astype(F32)

        def attend(i, _):
            rows = pl.ds(pl.multiple_of(i * TILE, TILE), TILE)
            q2 = split_heads(proj_ref[rows, cols.q : cols.q + LANES], q_low)
            d_out = dcore[rows, width : width + LANES]
            do2 = split_heads(d_out, q_low)
            both = d_out.astype(F32) * lows_ref[rows, width : width + LANES].astype(F32)
            high = lax.Precision.HIGHEST
            deltas = [
                lax.dot_general(
                    pick, both, (((1,), (1,)), ((), ())), precision=high, preferred_element_type=F32
                )[0:1, :]
                for pick in (pick_low, pick_high)
            ]
            delta = jnp.concatenate(deltas, axis=1)
            lse = lse_ref[i][0:1, :]

            def piece_of(j, dq, masked):
                keys = pl.ds(pl.multiple_of(j * TILE, TILE), TILE)
                kk = proj_ref[keys, cols.k : cols.k + LANES]
                p = jnp.exp(nt(kk, q2) - lse)
                if masked:
                    p = jnp.where(diagonal, p, 0.0)
                ds = (p * (nt(proj_ref[keys, cols.v : cols.v + LANES], do2) - delta)).astype(B16)
                dv_sum[keys, :] += nn(p.astype(B16), do2)
                dk_sum[keys, :] += nn(ds, q2)
                return dq + tn(kk, ds)

            dq = jnp.zeros((LANES, 2 * TILE), F32)
            dq = lax.fori_loop(0, i, lambda j, c: piece_of(j, c, False), dq)
            dq = piece_of(i, dq, True)
            joined = jnp.concatenate([dq[:HD, :TILE], dq[HD:, TILE:]], axis=0) * HD**-0.5
            dproj_ref[rows, cols.q : cols.q + LANES] = joined.T.astype(B16)
            return 0

        lax.fori_loop(0, length // TILE, attend, 0)
        dproj_ref[:, cols.k : cols.k + LANES] = dk_sum[...].astype(B16)
        dproj_ref[:, cols.v : cols.v + LANES] = dv_sum[...].astype(B16)

    def scan_all():
        ri, ci = iotas(STEP, STEP)
        upper = ri <= ci
        tril = (ri >= ci).astype(F32)
        triu = upper.astype(F32)
        low_lanes = ci < HD
        decay = jnp.exp(few_ref[layer, 0, 2:3, :LANES])
        bias = few_ref[layer, 0, 3:4, :LANES]
        skips = skip_lanes(few_ref, layer, width)
        row, lane = iotas(width, LANES)
        group = ((row >> 6) == lane).astype(B16)
        grad_state[...] = jnp.zeros_like(grad_state)
        skip_sum[...] = jnp.zeros_like(skip_sum)
        heads_ref[...] = jnp.zeros_like(heads_ref)
        zero_rows = jnp.zeros((STEP - 2 * cols.pairs, LANES), F32)

        def scan_block(back, _):
            b = blocks - 1 - back
            rows = pl.ds(pl.multiple_of(b * STEP, STEP), STEP)
            raw = step_ref[rows, :] + bias
            dt = softplus(raw)
            a = -dt * decay
            run = exact(tril, a)
            run_t = run.T
            bm = proj_ref[rows, cols.b : cols.b + LANES]
            cm = proj_ref[rows, cols.c : cols.c + LANES]
            cbt = jnp.where(upper, nt(bm, cm), 0.0)
            low_state = states_ref[b]
            grads_out = grad_state[...]
            low_grad = grads_out.astype(B16)
            carried = nn(cm, low_state)
            pulled = nn(bm, low_grad)
            dcb = jnp.zeros((STEP, STEP), F32)
            dy_fades, u_tails, fades = [], [], []
            carry_terms, direct_terms, tail_terms = [], [], []
            row_sums = []
            col_sums = jnp.zeros((STEP, LANES), F32)
            for p in range(cols.pairs):
                lanes = slice(LANES * p, LANES * (p + 1))
                u16 = proj_ref[rows, cols.u + LANES * p : cols.u + LANES * (p + 1)]
                u = u16.astype(F32)
                z = proj_ref[rows, cols.z + LANES * p : cols.z + LANES * (p + 1)].astype(F32)
                y = y_ref[rows, lanes].astype(F32)
                dm = dcore[rows, lanes].astype(F32)
                sg = sigmoid(z)
                dy = dm * z * sg
                dproj_ref[rows, cols.z + LANES * p : cols.z + LANES * (p + 1)] = (
                    dm * y * sg * (1.0 + z * (1.0 - sg))
                ).astype(B16)
                dy16 = dy.astype(B16)
                skip_sum[:, lanes] += u * dy
                run_b = [spread(run, 2 * p + k, STEP) for k in range(2)]
                dt_b = [spread(dt, 2 * p + k, STEP) for k in range(2)]
                run_w = jnp.where(low_lanes, run_b[0], run_b[1])
                dt_w = jnp.where(low_lanes, dt_b[0], dt_b[1])
                end = run_w[STEP - 1 : STEP, :]
                fade = jnp.exp(run_w)
                tail = jnp.exp(end - run_w)
                dmix = nt(split_heads(u16, low_lanes), dy16)
                mixes = []
                for k in range(2):
                    gap = jnp.exp(jnp.minimum(run_t[2 * p + k : 2 * p + k + 1, :] - run_b[k], 0.0))
                    mixes.append((gap * cbt).astype(B16))
                    weighted = gap * dt_b[k] * dmix[STEP * k : STEP * (k + 1), :]
                    dcb += weighted
                    moved = weighted * cbt
                    row_sums.append(jnp.sum(moved, axis=0, keepdims=True))
                    col_sums = jnp.where(
                        ci == 2 * p + k, jnp.sum(moved, axis=1, keepdims=True), col_sums
                    )
                inside = nn(jnp.concatenate(mixes, axis=1), split_heads(dy16, low_lanes))
                pull_tail = tail * pulled[:, lanes]
                g = inside + pull_tail
                dproj_ref[rows, cols.u + LANES * p : cols.u + LANES * (p + 1)] = (
                    dt_w * g + skips[:, lanes] * dy
                ).astype(B16)
                dy_fade = dy * fade
                dy_fades.append(dy_fade.astype(B16))
                u_tails.append((u * dt_w * tail).astype(B16))
                fades.append(jnp.exp(end))
                carry_terms.append((dy_fade * carried[:, lanes]).astype(B16))
                direct_terms.append((u * g).astype(B16))
                tail_terms.append((u * pull_tail).astype(B16))
            dy_fade = jnp.concatenate(dy_fades, axis=1)
            dcb = jnp.where(upper, dcb, 0.0).astype(B16)
            dproj_ref[rows, cols.c : cols.c + LANES] = (tn(dcb, bm) + nt(dy_fade, low_state)).astype(B16)
            dproj_ref[rows, cols.b : cols.b + LANES] = (
                nn(dcb, cm) + nt(jnp.concatenate(u_tails, axis=1), low_grad)
            ).astype(B16)
            carry_term = nn(jnp.concatenate(carry_terms, axis=1), group)
            direct_term = nn(jnp.concatenate(direct_terms, axis=1), group)
            tail_term = dt * nn(jnp.concatenate(tail_terms, axis=1), group)
            overlap = jnp.sum(low_state.astype(F32) * grads_out, axis=0, keepdims=True)
            overlap = exact(jnp.broadcast_to(overlap, (8, width)), group.astype(F32))[0:1, :]
            overlap = overlap * jnp.exp(run[STEP - 1 : STEP, :])
            row_sum = jnp.concatenate(row_sums + [zero_rows], axis=0).T
            d_run = row_sum - col_sums + carry_term - tail_term
            d_a = exact(triu, d_run) + (jnp.sum(tail_term, axis=0, keepdims=True) + overlap)
            d_step = (direct_term - decay * d_a) * sigmoid(raw)
            dproj_ref[rows, cols.step : cols.step + LANES] = d_step.astype(B16)
            heads_ref[0:1, :] += jnp.sum(d_a * a, axis=0, keepdims=True)
            heads_ref[1:2, :] += jnp.sum(d_step, axis=0, keepdims=True)
            grad_state[...] = grads_out * jnp.concatenate(fades, axis=1) + tn(cm, dy_fade)
            return 0

        lax.fori_loop(0, blocks, scan_block, 0)
        skip = jnp.sum(skip_sum[...], axis=0, keepdims=True)
        heads_ref[2:3, :] = exact(jnp.broadcast_to(skip, (8, width)), group.astype(F32))[0:1, :]

    def back_all():
        multiply_back(
            dproj_ref, weights_ref, at_row.inner, cols.q // piece, part_ref, rows_ref, gain_sum, r.rest
        )

    def shared_all():
        wide = cols.total - cols.b
        member = lax.axis_index(TENSOR)
        heads = q_heads[1]
        group = member * q_heads[0] // (HA // KVH)
        source, target = iotas(wide, wide)
        kind = source >> 7
        wanted = jnp.where(
            kind < 2,
            source,
            jnp.where(
                kind < 4,
                2 * NS + (kind - 2) * KVH * HD + group * HD + (source & (HD - 1)),
                source + member * heads,
            ),
        )
        fold = ((target == wanted) & (source < 4 * LANES + heads)).astype(B16)

        def fold_rows(i, _):
            rows = pl.ds(pl.multiple_of(i * TILE, TILE), TILE)
            folded[rows, :] = nn(dproj_ref[rows, cols.b :], fold).astype(B16)
            return 0

        lax.fori_loop(0, length // TILE, fold_rows, 0)
        sub = piece // members
        half = sub // 2
        lane = iotas(piece, LANES)[1]
        head_lane = iotas(8, LANES)[1]
        shifted = jnp.where(
            (head_lane >= HEADS_AT) & (head_lane < HEADS_AT + heads),
            pltpu.roll(heads_ref[...], HEADS_AT, 1),
            0.0,
        )
        for k in range(ways):
            at = slice(k * piece, (k + 1) * piece)
            grad = tn(rows_ref[:, at], folded[...])
            columns = []
            for row, sums in ((0, gain_sum), (1, r.gain_ffn)):
                gain = few_ref[layer, k, row : row + 1, :]
                columns.append(jnp.broadcast_to(sums[0:1, at] / gain, (LANES, piece)).T)
            last = grad[:, wide - LANES :]
            last = jnp.where(lane == GAINS_AT, columns[0], last)
            last = jnp.where(lane == GAINS_AT + 1, columns[1], last)
            for t in range(members):
                for h in range(2):
                    to = t * (depth // members) + (h * ways + k) * half
                    rows = slice(t * sub + h * half, t * sub + (h + 1) * half)
                    staged[to : to + half, : wide - LANES] = grad[rows, : wide - LANES]
                    staged[to : to + half, wide - LANES :] = last[rows, :]
            to = pl.multiple_of(member * (depth // members) + k * half, 8)
            staged[pl.ds(to, 8), wide - LANES :] += shifted
        part_ref[:, depth:] = staged[...].astype(B16)

    return [into_all, attend_all, scan_all, back_all, shared_all]


def ffn_fwd_phases(r, at=0):
    rows_ref, weights_ref, gu_ref, hidden_ref = r.rows_ffn, r.gates, r.gu, r.hidden
    units = hidden_ref.shape[1]
    piece = weights_ref.shape[2]
    count = units // piece

    def up(i, _):
        rows = pl.ds(pl.multiple_of(i * TILE, TILE), TILE)
        for c in range(count):
            at = slice(c * piece, (c + 1) * piece)
            g = blocks_nn(rows_ref, rows, weights_ref, c)
            v = blocks_nn(rows_ref, rows, weights_ref, c + count)
            gu_ref[rows, at] = g.astype(B16)
            gu_ref[rows, units + c * piece : units + (c + 1) * piece] = v.astype(B16)
            hidden_ref[rows, at] = (g * sigmoid(g) * v).astype(B16)
        return 0

    def up_all():
        lax.fori_loop(0, rows_ref.shape[0] // TILE, up, 0)

    def down_all():
        multiply_out(hidden_ref, weights_ref, 2 * units, r.part, at)

    return [up_all, down_all]


def ffn_bwd_phases(r):
    out_ref, weights_ref, gu_ref, dgu_ref = r.rows_out, r.gates, r.gu, r.dgu
    ways, _, piece = weights_ref.shape
    units = gu_ref.shape[1] // 2
    down_rows = slice(2 * units, 3 * units)

    def down(i, _):
        rows = pl.ds(pl.multiple_of(i * TILE, TILE), TILE)
        dh = nt(out_ref[rows, 0:piece], weights_ref[0, down_rows, :])
        for k in range(1, ways):
            dh += nt(out_ref[rows, k * piece : (k + 1) * piece], weights_ref[k, down_rows, :])
        g = gu_ref[rows, :units].astype(F32)
        v = gu_ref[rows, units:].astype(F32)
        sg = sigmoid(g)
        dgu_ref[rows, :units] = (dh * v * sg * (1.0 + g * (1.0 - sg))).astype(B16)
        dgu_ref[rows, units:] = (dh * g * sg).astype(B16)
        return 0

    def down_all():
        lax.fori_loop(0, out_ref.shape[0] // TILE, down, 0)

    def back_all():
        multiply_back(
            dgu_ref, weights_ref, 0, 2 * units // piece, r.part, r.rows_ffn, r.gain_ffn
        )

    return [down_all, back_all]


def grad_columns(rows_ref, grad_ref, out_ref):
    _, ways, half, width = out_ref.shape
    for k in range(ways):
        block = rows_ref[:, 2 * half * k : 2 * half * (k + 1)]
        for first in range(0, width, 512):
            last = min(first + 512, width)
            value = tn(block, grad_ref[:, first:last]).astype(B16)
            out_ref[0, k, :, first:last] = value[:half, :]
            out_ref[1, k, :, first:last] = value[half:, :]


def grad_rows(lows_ref, back_ref, out_ref):
    _, ways, half, piece = out_ref.shape
    for h in range(2):
        block = lows_ref[:, h * half : (h + 1) * half]
        for k in range(ways):
            out_ref[h, k] = tn(block, back_ref[:, k * piece : (k + 1) * piece]).astype(B16)


DMA = pltpu.SemaphoreType.DMA
MESH = pl.DeviceIdType.MESH
PIPE, DP, TENSOR = "pipe", "dp", "tensor"

BEGIN, SENT, CHUNK, SPREAD, GIVEN, END = -1, 20, 30, 40, 50, 60


class Bag:
    def __init__(self, **entries):
        self.__dict__.update(entries)

    def add(self, other):
        self.__dict__.update(other.__dict__)


def remote(source, target, send, receive, device):
    return pltpu.make_async_remote_copy(
        src_ref=source, dst_ref=target, send_sem=send, recv_sem=receive,
        device_id=device, device_id_type=MESH,
    )


class Helper:
    def __init__(self, when):
        self.when = when
        self.inputs, self.outs, self.scratch = [], [], []
        self.results = None

    @property
    def result(self):
        return self.results[0]


def cross_devices(ways):
    section, place = lax.axis_index(PIPE), lax.axis_index(DP)
    return [{PIPE: 1 - section}] + [{DP: (place + k) % ways} for k in range(1, ways)]


class Few(Helper):
    def __init__(self, ways, shard, when):
        super().__init__(when)
        self.ways = ways
        self.inputs = [shard]
        self.outs = [((2, ways) + shard.shape, F32, pltpu.VMEM)]
        self.scratch = [DMA((1,)), DMA((1,)), DMA((2, ways)), DMA((2, ways)), DMA((1,))]

    def bind(self, r, inputs, outs, scratch):
        (shard,), (few,) = inputs, outs
        r.few = few
        section, place, ways = lax.axis_index(PIPE), lax.axis_index(DP), self.ways
        pair_send, pair_recv, line_send, line_recv, local = scratch
        mine = few.at[section, place]

        def over():
            return remote(shard, mine, pair_send.at[0], pair_recv.at[0], {PIPE: 1 - section})

        def line(layer, k, there):
            block = few.at[layer, there]
            return remote(
                block, block, line_send.at[layer, k], line_recv.at[layer, k], {DP: (place + k) % ways}
            )

        def start():
            over().start()
            own = pltpu.make_async_copy(shard, mine, local.at[0])
            own.start()
            own.wait()

        def spread():
            over().wait_recv()
            for layer in range(2):
                for k in range(1, ways):
                    line(layer, k, place).start()

        def finish():
            for layer in range(2):
                for k in range(1, ways):
                    line(layer, k, (place + ways - k) % ways).wait_recv()
            over().wait_send()
            for layer in range(2):
                for k in range(1, ways):
                    line(layer, k, place).wait_send()

        return [start, spread, finish]


class Cargo(Helper):
    CHUNKS = 4

    def __init__(self, layer, ways, shard, when, members=0, shared=0):
        super().__init__(when)
        self.layer, self.ways, self.rows = layer, ways, shard.shape[0]
        self.members, self.shared = members, shared
        n = self.CHUNKS
        self.first = (self.rows * 2 // 5 + 8 * n) // (16 * n) * (16 * n)
        self.inputs = [shard]
        self.outs = [((ways,) + shard.shape, shard.dtype, pl.ANY)]
        self.scratch = [DMA((n,)), DMA((n,))] + [DMA((ways, n))] * 6 + [DMA((1,))]
        if shared:
            self.outs.append(((members, ways, shared, shard.shape[1]), shard.dtype, pl.ANY))
            self.scratch += [DMA((members,))] * 4 + [DMA((1,))]

    def bind(self, r, inputs, outs, scratch):
        (shard_ref,), out_ref = inputs, outs[0]
        early_send, early_recv, up_send, up_recv, down_send, down_recv, over_send, over_recv, local = scratch[:9]
        section, place = lax.axis_index(PIPE), lax.axis_index(DP)
        partner = {PIPE: 1 - section}
        ways, chunks = self.ways, self.CHUNKS
        sizes = {True: self.first // chunks, False: (self.rows - self.first) // chunks}

        def by_role(step):
            def both():
                pl.when(section == self.layer)(lambda: step(True))
                pl.when(section != self.layer)(lambda: step(False))

            return both

        def part(owner, c):
            return pl.ds((0 if owner else self.first) + c * sizes[owner], sizes[owner])

        def early(c):
            at = part(False, c)
            return remote(
                shard_ref.at[at, :], out_ref.at[place, at, :], early_send.at[c], early_recv.at[c], partner
            )

        def line(owner, up, hop, c):
            at = part(owner, c)
            send, receive = (up_send, up_recv) if up else (down_send, down_recv)
            shard = place - hop if up else place + hop
            source = shard_ref if owner and hop == 0 else out_ref.at[shard]
            return remote(
                source.at[at, :], out_ref.at[shard, at, :], send.at[hop, c], receive.at[hop, c],
                {DP: (place + (1 if up else ways - 1)) % ways},
            )

        def sends(up, hop):
            if up:
                return (place >= hop) & (place < ways - 1)
            return (place < ways - hop) & (place > 0)

        def over(owner, shard, c, own=False):
            at = part(owner, c)
            source = shard_ref if own else out_ref.at[shard]
            return remote(
                source.at[at, :], out_ref.at[shard, at, :], over_send.at[shard, c], over_recv.at[shard, c],
                partner,
            )

        def own_copy():
            return pltpu.make_async_copy(shard_ref, out_ref.at[place], local.at[0])

        def launch(owner, c):
            for up in (True, False):
                pl.when(sends(up, 0))(lambda up=up: line(owner, up, 0, c).start())

        def start(owner):
            if owner:
                for c in range(chunks):
                    early(c).start()
                    launch(True, c)
                for c in range(chunks):
                    over(True, place, c, True).start()
                own_copy().start()

        def spread(c, owner):
            if not owner:
                early(c).wait_recv()
                launch(False, c)

        def hop(count, c, owner):
            for up in (True, False):
                shard = place - count if up else place + count

                @pl.when(shard >= 0 if up else shard < ways)
                def _(up=up, shard=shard):
                    line(owner, up, count - 1, c).wait_recv()
                    if count < ways - 1:
                        pl.when(sends(up, count))(lambda: line(owner, up, count, c).start())
                    over(owner, shard, c).start()

        def wait_over(owner, c):
            for shard in range(ways):

                def wait(shard=shard):
                    block = out_ref.at[shard, part(not owner, c), :]
                    remote(
                        block, block, over_send.at[shard, c], over_recv.at[shard, c], partner
                    ).wait_recv()

                if owner:
                    pl.when(place != shard)(wait)
                else:
                    wait()

        first_waited = 1 if self.shared else 0

        def finish(owner):
            for c in range(chunks):
                if owner or c >= first_waited:
                    wait_over(owner, c)
            for c in range(chunks):
                if owner:
                    early(c).wait_send()
                for count in range(ways - 1):
                    for up in (True, False):
                        pl.when(sends(up, count))(
                            lambda up=up, count=count: line(owner, up, count, c).wait_send()
                        )
                for shard in range(ways):

                    def wait(shard=shard):
                        over(owner, shard, c).wait_send()

                    if owner:
                        wait()
                    else:
                        pl.when(place != shard)(wait)
            if owner and not self.shared:
                own_copy().wait()

        steps = [start]
        steps += [functools.partial(spread, c) for c in range(chunks)]
        steps += [functools.partial(hop, count, c) for count in range(1, ways) for c in range(chunks)]
        steps = [by_role(step) for step in steps]
        if not self.shared:
            return steps + [by_role(finish)]

        assert self.shared <= sizes[True]
        all_ref = outs[1]
        give_send, give_recv, far_send, far_recv, keep = scratch[9:]
        me = lax.axis_index(TENSOR)
        pairs = self.members // 2
        mine, side = me // 2, me % 2
        sibling = 2 * mine + 1 - side
        share = out_ref.at[:, pl.ds(0, self.shared), :]

        def far(count):
            return 2 * ((mine + count) % pairs) + side

        def across(count):
            return 2 * ((mine + count) % pairs) + 1 - side

        def give(count):
            block = all_ref.at[far(count)]
            return remote(
                share if count == 0 else block, block, give_send.at[count], give_recv.at[count],
                {TENSOR: sibling},
            )

        def send_far(count, slot):
            return remote(
                share, all_ref.at[me], far_send.at[count], far_recv.at[slot], {TENSOR: far(count)}
            )

        def own_share():
            return pltpu.make_async_copy(share, all_ref.at[me], keep.at[0])

        def share_out():
            pl.when(section != self.layer)(lambda: wait_over(False, 0))
            pl.when(section == self.layer)(lambda: own_copy().wait())
            for count in range(1, pairs):
                send_far(count, pairs - count).start()
            give(0).start()
            own_share().start()

        def pass_on():
            for count in range(1, pairs):
                send_far(count, count).wait_recv()
                give(count).start()

        def finish_all():
            by_role(finish)()
            for count in range(pairs):
                block = all_ref.at[sibling if count == 0 else across(count)]
                remote(
                    block, block, give_send.at[count], give_recv.at[count], {TENSOR: sibling}
                ).wait_recv()
            for count in range(pairs):
                give(count).wait_send()
                if count:
                    send_far(count, pairs - count).wait_send()
            own_share().wait()

        at = len(steps) - (chunks - 1)
        return steps[:at] + [share_out] + steps[at:] + [pass_on, finish_all]


class Haul(Helper):
    def __init__(self, layer, ways, sources, specs, when, swap=True, line=True):
        super().__init__(when)
        self.layer, self.ways, self.sources, self.swap, self.line = layer, ways, sources, swap, line
        self.count = len(specs)
        self.order = sorted(range(1, ways), key=lambda k: abs(2 * k - ways)) + [0]
        for (_, blocks, rows, columns), dtype in specs:
            block = pltpu.VMEM((blocks, rows, columns), dtype)
            if swap and not line:
                self.outs.append(((blocks, rows, columns), dtype, pltpu.VMEM))
            if line:
                self.outs.append(((2, rows, columns), dtype, pltpu.VMEM))
            if swap:
                self.scratch += [block, DMA((ways,)), DMA((ways,))]
            if swap and line:
                self.scratch.append(block)
            if line:
                self.scratch += [block, pltpu.VMEM((rows, columns), dtype), DMA((ways,)), DMA((ways,))]
                self.scratch += [DMA((1,)), DMA((1,))]

    def bind(self, r, inputs, outs, scratch):
        section, place, ways = lax.axis_index(PIPE), lax.axis_index(DP), self.ways
        partner = {PIPE: 1 - section}
        scratch = list(scratch)
        arrays = []
        for source, out in zip(self.sources, outs):
            a = Bag(out=out)
            a.sent, a.read = source(r)
            a.sums = a.read
            if self.swap:
                a.swapped, a.swap_send, a.swap_recv = [scratch.pop(0) for _ in range(3)]
                a.sums = scratch.pop(0) if self.line else out
                a.sums_sent = a.sums
            else:
                a.sums_sent = a.sent
            if self.line:
                a.arrived, a.result, a.line_send, a.line_recv, a.last_send, a.last_recv = [
                    scratch.pop(0) for _ in range(6)
                ]
            arrays.append(a)

        def to(k):
            return (place + k) % ways

        def swap(a, k):
            return remote(
                a.sent.at[1 - section, to(k)], a.swapped.at[to(k)], a.swap_send.at[k], a.swap_recv.at[k],
                partner,
            )

        def line(a, k):
            return remote(
                a.sums_sent.at[to(k)], a.arrived.at[k], a.line_send.at[k], a.line_recv.at[k], {DP: to(k)}
            )

        def last(a):
            return remote(
                a.result, a.out.at[1 - self.layer], a.last_send.at[0], a.last_recv.at[0], partner
            )

        def start():
            for k in self.order:
                for a in arrays:
                    if self.swap:
                        swap(a, k).start()
                    elif k:
                        line(a, k).start()

        def fold(k):
            def step():
                for a in arrays:
                    swap(a, k).wait_recv()
                    total = a.read[section, to(k)].astype(F32) + a.swapped[to(k)].astype(F32)
                    a.sums[to(k)] = total.astype(a.sums.dtype)
                    if k and self.line:
                        line(a, k).start()

            return step

        def reduce():
            for a in arrays:
                total = a.sums[place].astype(F32)
                for k in range(1, ways):
                    line(a, k).wait_recv()
                    total += a.arrived[k].astype(F32)
                a.result[...] = total.astype(a.out.dtype)

            @pl.when(section == self.layer)
            def _():
                for a in arrays:
                    a.out[self.layer] = a.result[...]

            @pl.when(section != self.layer)
            def _():
                for a in arrays:
                    last(a).start()

        def finish():
            if self.line:

                @pl.when(section == self.layer)
                def _():
                    for a in arrays:
                        last(a).wait_recv()

                @pl.when(section != self.layer)
                def _():
                    for a in arrays:
                        last(a).wait_send()
                        a.out[...] = jnp.zeros_like(a.out)

            for k in self.order:
                for a in arrays:
                    if self.swap:
                        swap(a, k).wait_send()
                    if k and self.line:
                        line(a, k).wait_send()

        steps = [start]
        if self.swap:
            steps += [fold(k) for k in self.order]
        if self.line:
            steps.append(reduce)
        return steps + [finish]


class Straight(Helper):
    def __init__(self, layer, ways, source, spec, when):
        super().__init__(when)
        self.layer, self.ways, self.source = layer, ways, source
        (_, blocks, rows, columns), dtype = spec
        result = (2, rows, columns)
        self.outs = [(result, dtype, pltpu.VMEM)]
        self.scratch = [pltpu.VMEM((blocks,) + result, dtype), pltpu.VMEM(result, dtype)]
        self.scratch += [pltpu.VMEM(result, dtype), DMA((2, ways)), DMA((2, ways)), DMA((1,)), DMA((1,))]

    def bind(self, r, inputs, outs, scratch):
        sent, read = self.source(r)
        (out,) = outs
        arrived, result, handed, line_send, line_recv, last_send, last_recv = scratch
        section, place, ways = lax.axis_index(PIPE), lax.axis_index(DP), self.ways
        order = sorted(range(1, ways), key=lambda k: abs(2 * k - ways))

        def line(half, k):
            to = (place + k) % ways
            return remote(
                sent.at[half, to], arrived.at[k, half], line_send.at[half, k], line_recv.at[half, k], {DP: to}
            )

        def last():
            return remote(result, handed, last_send.at[0], last_recv.at[0], {PIPE: 1 - section})

        def start():
            for k in order:
                for half in range(2):
                    line(half, k).start()

        def reduce():
            for half in range(2):
                total = read[half, place].astype(F32)
                for k in range(1, ways):
                    line(half, k).wait_recv()
                    total += arrived[k, half].astype(F32)
                result[half] = total.astype(result.dtype)

            @pl.when(section != self.layer)
            def _():
                last().start()

        def finish():
            @pl.when(section == self.layer)
            def _():
                last().wait_recv()
                out[...] = (result[...].astype(F32) + handed[...].astype(F32)).astype(out.dtype)

            @pl.when(section != self.layer)
            def _():
                last().wait_send()
                out[...] = jnp.zeros_like(out)

            for k in order:
                for half in range(2):
                    line(half, k).wait_send()

        return [start, reduce, finish]


class Place(Helper):
    PIECES = 4

    def __init__(self, source, shape, late, when):
        super().__init__(when)
        self.source, self.late, self.size = source, late, shape[0] // self.PIECES
        self.outs = [((2,) + shape, B16, pl.ANY)]
        self.scratch = [DMA((self.PIECES,)), DMA((self.PIECES,)), DMA((self.PIECES,))]

    def bind(self, r, inputs, outs, scratch):
        (out,) = outs
        send, receive, local = scratch
        section = lax.axis_index(PIPE)
        rows = self.source(r)

        def over(layer, c):
            at = pl.ds(c * self.size, self.size)
            return remote(
                rows[layer].at[at, :], out.at[1 - layer, at, :], send.at[c], receive.at[c], {PIPE: 1 - section}
            )

        def own(layer, c):
            at = pl.ds(c * self.size, self.size)
            return pltpu.make_async_copy(rows[layer].at[at, :], out.at[layer, at, :], local.at[c])

        def hand(layer, c):
            pl.when(section != layer)(lambda: over(layer, c).start())
            pl.when(section == layer)(lambda: own(layer, c).start())

        def early():
            for c in range(self.PIECES):
                hand(1 - self.late, c)

        def finish():
            for c in range(self.PIECES):
                for layer in range(2):

                    @pl.when(section == layer)
                    def _(layer=layer):
                        over(1 - layer, c).wait()
                        own(layer, c).wait()

        return [early] + [functools.partial(hand, self.late, c) for c in range(self.PIECES)] + [finish]


def exchange_kernel(plan, *refs):
    refs = list(refs)

    def take(count):
        return [refs.pop(0) for _ in range(count)]

    r = Bag(raw=Bag())
    held = {}
    for name in plan.inputs:
        held[name] = take(1)[0]
    r.raw = Bag(**held)
    helper_inputs = [take(len(h.inputs)) for h in plan.helpers]
    targets = {name: take(1)[0] for name in plan.outs}
    gathered = take(len(plan.gathers))
    helper_outs = [take(len(h.outs)) for h in plan.helpers]
    loaded = [name for name in plan.inputs if plan.need(name) is not None]
    for name in loaded:
        setattr(r, name, take(1)[0])
    for name in plan.outs:
        setattr(r, name, take(1)[0])
    for name in plan.scratch:
        setattr(r, name, take(1)[0])
    load_sem, store_sem = take(2)
    if plan.scatter:
        part_ref, pair_in, far_out, far_in, pair_send, pair_recv, far_send, far_recv = take(8)
        r.part = part_ref
    if plan.gathers:
        mine_refs = take(len(plan.gathers))
        give_send, give_recv, spread_send, spread_recv, keep_sem = take(5)
    helpers = []
    for h, inputs, outs in zip(plan.helpers, helper_inputs, helper_outs):
        helpers.append((h.bind(r, inputs, outs, take(len(h.scratch))), h.when))

    members, pieces = plan.members, plan.pieces
    pairs = members // 2
    me = lax.axis_index(TENSOR)
    mine, side = me // 2, me % 2
    sibling = 2 * mine + 1 - side
    size = plan.rows // pieces

    def far(k):
        return 2 * ((mine + k) % pairs) + side

    def across(k):
        return 2 * ((mine + k) % pairs) + 1 - side

    def rows_of(member, c):
        return pl.ds(pl.multiple_of(member * plan.rows + c * size, size), size)

    def chunk(c):
        return pl.ds(c * size, size)

    def copy(source, target, send, receive, member):
        return remote(source, target, send, receive, {TENSOR: member})

    loads = {}
    for i, name in enumerate(sorted(loaded, key=plan.need)):
        loads[name] = pltpu.make_async_copy(held[name], getattr(r, name), load_sem.at[i])
        loads[name].start()

    def arrive(stage):
        for name in list(loads):
            if plan.need(name) <= stage:
                loads.pop(name).wait()

    stores = []

    def flush(stage):
        for i, name in enumerate(plan.outs):
            if plan.done(name) == stage:
                store = pltpu.make_async_copy(getattr(r, name), targets[name], store_sem.at[i])
                store.start()
                stores.append(store)

    def point(stage):
        for steps, when in helpers:
            count = len(steps) if stage == END else when.get(stage, 0)
            for _ in range(min(count, len(steps))):
                steps.pop(0)()
        flush(stage)

    def run_fill(i):
        if i < len(plan.fills):
            plan.fills[i](r)

    barrier = pltpu.get_barrier_semaphore()
    greeted = [{TENSOR: sibling}] + [{TENSOR: far(k)} for k in range(1, pairs)]
    if helpers:
        greeted += cross_devices(plan.ways)
    for device in greeted:
        pl.semaphore_signal(barrier, inc=1, device_id=device, device_id_type=MESH)
    pl.semaphore_wait(barrier, len(greeted))

    arrive(BEGIN)
    point(BEGIN)
    for i, phase in enumerate(plan.phases(r) if plan.phases else []):
        arrive(i)
        phase()
        point(i)

    if plan.scatter:
        to_pair = {}
        for c in range(pieces):
            for k in range(1, pairs):
                to_pair[k, c] = copy(
                    part_ref.at[rows_of(across(k), c), :], pair_in.at[k, chunk(c), :],
                    pair_send.at[k, c], pair_recv.at[k, c], sibling,
                )
                to_pair[k, c].start()
        for c in range(pieces):
            to_pair[0, c] = copy(
                part_ref.at[rows_of(sibling, c), :], pair_in.at[0, chunk(c), :],
                pair_send.at[0, c], pair_recv.at[0, c], sibling,
            )
            to_pair[0, c].start()
        to_far = {}
        for c in range(pieces):
            for k in range(1, pairs):
                to_pair[k, c].wait_recv()
                far_out[k - 1, chunk(c), :] = (
                    part_ref[rows_of(far(k), c), :].astype(F32)
                    + pair_in[k, chunk(c), :].astype(F32)
                ).astype(B16)
                to_far[k, c] = copy(
                    far_out.at[k - 1, chunk(c), :], far_in.at[pairs - k - 1, chunk(c), :],
                    far_send.at[k - 1, c], far_recv.at[pairs - k - 1, c], far(k),
                )
                to_far[k, c].start()
    arrive(SENT)
    if plan.scatter:
        run_fill(0)
    point(SENT)

    given, spreads, keeps = {}, {}, []
    for c in range(pieces):
        total = None
        if plan.scatter:
            to_pair[0, c].wait_recv()
            total = part_ref[rows_of(me, c), :].astype(F32) + pair_in[0, chunk(c), :].astype(F32)
            for k in range(1, pairs):
                copy(
                    far_out.at[k - 1, chunk(c), :], far_in.at[k - 1, chunk(c), :],
                    far_send.at[k - 1, c], far_recv.at[k - 1, c], far(k),
                ).wait_recv()
                total += far_in[k - 1, chunk(c), :].astype(F32)
        results = plan.work(r, c, chunk(c), total)
        for g, rows_ref in enumerate(gathered):
            own = mine_refs[g].at[chunk(c), :]
            there = rows_ref.at[rows_of(me, c), :]
            mine_refs[g][chunk(c), :] = results[g]
            for k in range(1, pairs):
                spreads[g, k, c] = copy(
                    own, there, spread_send.at[g, k - 1, c], spread_recv.at[g, pairs - k - 1, c], far(k)
                )
                spreads[g, k, c].start()
            given[g, 0, c] = copy(own, there, give_send.at[g, 0, c], give_recv.at[g, 0, c], sibling)
            given[g, 0, c].start()
            keeps.append(pltpu.make_async_copy(own, there, keep_sem.at[g, c]))
            keeps[-1].start()
        point(CHUNK + c)
    run_fill(1)
    point(SPREAD)
    for g, rows_ref in enumerate(gathered):
        for c in range(pieces):
            for k in range(1, pairs):
                block = rows_ref.at[rows_of(far(k), c), :]
                copy(
                    block, block, spread_send.at[g, k - 1, c], spread_recv.at[g, k - 1, c], far(k)
                ).wait_recv()
                given[g, k, c] = copy(
                    block, block, give_send.at[g, k, c], give_recv.at[g, k, c], sibling
                )
                given[g, k, c].start()
    point(GIVEN)
    for g, rows_ref in enumerate(gathered):
        for c in range(pieces):
            for k in range(pairs):
                block = rows_ref.at[rows_of(sibling if k == 0 else across(k), c), :]
                copy(block, block, give_send.at[g, k, c], give_recv.at[g, k, c], sibling).wait_recv()
        for c in range(pieces):
            for k in range(pairs):
                given[g, k, c].wait_send()
            for k in range(1, pairs):
                spreads[g, k, c].wait_send()
    if plan.scatter:
        for c in range(pieces):
            for k in range(pairs):
                to_pair[k, c].wait_send()
            for k in range(1, pairs):
                to_far[k, c].wait_send()
    arrive(END)
    point(END)
    for store in stores + keeps:
        store.wait()


def exchange(
    name, number, members, ways, rows, depth, work, inputs, outs=None, need=None, done=None, scratch=None,
    phases=None, fills=(), part_width=0, gathers=None, helpers=(), pieces=4,
):
    pairs = members // 2
    others = max(pairs - 1, 1)
    outs, scratch, need, done = outs or {}, scratch or {}, need or {}, done or {}
    gathers = gathers or []
    hbm, vmem = pl.BlockSpec(memory_space=pl.ANY), pl.BlockSpec(memory_space=pltpu.VMEM)
    plan = Bag(
        inputs=list(inputs), outs=list(outs), scratch=list(scratch), gathers=gathers, helpers=list(helpers),
        members=members, ways=ways, rows=rows, pieces=pieces, scatter=bool(part_width),
        phases=phases, fills=list(fills), work=work,
        need=lambda n: need.get(n, 0 if phases else BEGIN), done=lambda n: done.get(n, END),
    )
    staging = [pltpu.VMEM(a.shape, a.dtype) for n, a in inputs.items() if plan.need(n) is not None]
    staging += [pltpu.VMEM(*spec) for spec in outs.values()]
    staging += list(scratch.values())
    staging += [DMA((max(len(inputs), 1),)), DMA((max(len(outs), 1),))]
    if part_width:
        staging += [
            pltpu.VMEM((members * rows, part_width), B16),
            pltpu.VMEM((pairs, rows, part_width), B16),
            pltpu.VMEM((others, rows, part_width), B16),
            pltpu.VMEM((others, rows, part_width), B16),
            DMA((pairs, pieces)), DMA((pairs, pieces)), DMA((others, pieces)), DMA((others, pieces)),
        ]
    count = len(gathers)
    if count:
        staging += [pltpu.VMEM((rows, depth), B16)] * count
        staging += [
            DMA((count, pairs, pieces)), DMA((count, pairs, pieces)),
            DMA((count, others, pieces)), DMA((count, others, pieces)), DMA((count, pieces)),
        ]
    operands = list(inputs.values())
    shapes = [jax.ShapeDtypeStruct(*spec) for spec in outs.values()]
    shapes += [jax.ShapeDtypeStruct((members * rows, depth), B16)] * count
    spaces = [hbm] * len(shapes)
    for h in helpers:
        operands += h.inputs
        shapes += [jax.ShapeDtypeStruct(shape, dtype) for shape, dtype, _ in h.outs]
        spaces += [pl.BlockSpec(memory_space=space) for _, _, space in h.outs]
        staging += h.scratch
    results = pl.pallas_call(
        functools.partial(exchange_kernel, plan),
        out_shape=shapes,
        in_specs=[hbm] * len(operands),
        out_specs=spaces,
        scratch_shapes=staging,
        compiler_params=pltpu.CompilerParams(
            collective_id=number, has_side_effects=True, vmem_limit_bytes=VMEM_LIMIT
        ),
        cost_estimate=pl.CostEstimate(
            flops=20_000_000_000, bytes_accessed=50_000_000, transcendentals=0
        ),
        name=name,
    )(*operands)
    results = list(results)
    got = {n: results.pop(0) for n in list(outs) + list(gathers)}
    for h in helpers:
        h.results = [results.pop(0) for _ in h.outs]
    return Bag(**got)


def rms(rows, gain):
    scale = lax.rsqrt(jnp.mean(rows * rows, axis=-1, keepdims=True) + EPS)
    return rows * scale * gain


def rms_back(rows, gain, grad):
    scale = lax.rsqrt(jnp.mean(rows * rows, axis=-1, keepdims=True) + EPS)
    scaled = gain * grad
    mean = jnp.mean(scaled * rows, axis=-1, keepdims=True)
    return scale * scaled - rows * (scale * scale * scale * mean)


def gain_of(r, layer, row):
    ways = r.few.shape[1]
    return jnp.concatenate([r.few[layer, k, row : row + 1, :] for k in range(ways)], axis=1)


def layer_input(r, layer, at):
    if layer == 0:
        return r.acts_in[lax.axis_index(PIPE), at, :].astype(F32)
    return r.x[at, :].astype(F32)


def layer_cotangent(r, layer, at):
    if layer == 1:
        return r.out_grad[lax.axis_index(PIPE), at, :]
    return r.cotangent[at, :]


def work_first(r, c, at, total):
    return rms(layer_input(r, 0, at), gain_of(r, 0, 0)).astype(B16), layer_cotangent(r, 1, at)


def work_mid(layer, r, c, at, total):
    residual = layer_input(r, layer, at) + total
    r.residual[at, :] = residual
    return (rms(residual, gain_of(r, layer, 1)).astype(B16),)


def work_turn(r, c, at, total):
    out = (r.residual[at, :] + total).astype(B16)
    r.x[at, :] = out
    return (rms(out.astype(F32), gain_of(r, 1, 0)).astype(B16),)


def work_back_ffn(layer, r, c, at, total):
    depth = r.residual.shape[1]
    residual = r.residual[at, :]
    if layer == 1:
        r.last[at, :] = (residual + total[:, depth:]).astype(B16)
    grad = layer_cotangent(r, layer, at).astype(F32) + rms_back(
        residual, gain_of(r, layer, 1), total[:, :depth]
    )
    r.d_residual[at, :] = grad
    return (grad.astype(B16),)


def work_back_mix(layer, r, c, at, total):
    depth = r.d_residual.shape[1]
    step = rms_back(layer_input(r, layer, at), gain_of(r, layer, 0), total[:, :depth])
    grad = (r.d_residual[at, :] + step).astype(B16)
    r.x_grad[at, :] = grad
    _, ways, block, _ = r.shared.shape
    blocks = total.shape[0] // block
    for i in range(blocks):
        j = c * blocks + i
        r.shared[j // ways, j % ways] = total[i * block : (i + 1) * block, depth:]
    return (grad,)


def widen(block, axis, size):
    missing = size - block.shape[axis]
    if missing == 0:
        return block
    pads = [(0, 0)] * block.ndim
    pads[axis] = (0, missing)
    return jnp.pad(block, pads)


def on_device(
    acts_in, out_grad, mix_gain, w_mixer_in, w_query, w_shared, w_step, a_log, dt_bias, d_skip,
    w_mamba_out, w_attn_out, ffn_gain, w_gate_up, w_down,
):
    section = lax.axis_index(PIPE)
    member = lax.axis_index(TENSOR)
    members = lax.axis_size(TENSOR)
    dp = lax.axis_size(DP)
    heads = a_log.shape[1]
    real = heads * HD
    width = (heads + heads % 2) * HD
    q_real = w_query.shape[2]
    cols = Cols(width)
    units = w_gate_up.shape[3]
    rows, depth = acts_in.shape[1:]
    length = rows * members
    piece = depth // dp
    wide = cols.total - cols.b

    at_row = MixerRows(cols, members)
    q_heads = q_real // HD
    inner = jnp.concatenate(
        [widen(w_mixer_in[0, :, 0], 1, width), widen(w_mixer_in[0, :, 1], 1, width)], axis=1
    )
    share = lax.dynamic_slice_in_dim(w_shared[0], member * (piece // members), piece // members, 0)
    share = jnp.concatenate([share[:, at : at + LANES] for at in range(0, 4 * LANES, LANES)], axis=0)
    mixer_shard = jnp.concatenate(
        [fold_lanes(share)(piece), fold_lanes(widen(w_query[0], 1, LANES))(piece)]
        + [inner[:, at : at + piece] for at in range(0, 2 * width, piece)]
        + [widen(w_mamba_out[0], 0, width), widen(w_attn_out[0], 0, LANES)],
        axis=0,
    )
    steps = lax.dynamic_slice_in_dim(w_step[0], member * heads, heads, 1).T.astype(F32)
    ffn_shard = jnp.concatenate(
        [w_gate_up[0, :, j, at : at + piece] for j in range(2) for at in range(0, units, piece)]
        + [w_down[0]],
        axis=0,
    )
    few_shard = jnp.concatenate(
        [mix_gain.astype(F32), ffn_gain.astype(F32)]
        + [widen(row, 1, piece) for row in (a_log, dt_bias, d_skip)]
        + [jnp.zeros((3, piece), F32), widen(steps, 0, 8)],
        axis=0,
    )

    def run(name, number, work, inputs, outs, **more):
        return exchange(name, number, members, dp, rows, depth, work, inputs, outs, **more)

    half = piece // 2
    low_units = width + LANES
    block32, block16 = ((rows, depth), F32), ((rows, depth), B16)
    core_keeps = dict(
        proj=((length, cols.step), B16),
        step=((length, LANES), F32),
        y=((length, width), B16),
        lows=((length, low_units), B16),
        states=((length // STEP, NS, width), B16),
        lse=((length // TILE, 8, 2 * TILE), F32),
    )
    ffn_keeps = dict(gu=((length, 2 * units), B16), hidden=((length, units), B16))
    gu_spec, down_spec = ((2, dp, half, 2 * units), B16), ((2, dp, units // 2, piece), B16)
    cat_spec, out_spec = ((2, dp, half, cols.b), B16), ((2, dp, low_units // 2, piece), B16)
    shared_spec = ((2, dp, half // members, wide), F32)
    gain_row = ((8, depth), F32)
    fills_ffn = [
        lambda r: grad_columns(r.rows_ffn, r.dgu, r.g_gu),
        lambda r: grad_rows(r.hidden, r.rows_out, r.g_down),
    ]
    fill_cat = lambda r: grad_columns(r.rows_mix, r.dproj, r.g_cat)
    fill_out = lambda r: grad_rows(r.lows, r.rows_back, r.g_out)

    load = Cargo(
        0, dp, mixer_shard,
        {BEGIN: 1, SENT: 2, CHUNK: 1, CHUNK + 1: 1, CHUNK + 2: 2, CHUNK + 3: 2, SPREAD: 2, GIVEN: 4},
        members, at_row.shared,
    )
    few = Few(dp, few_shard, {BEGIN: 3})
    got = run(
        "first", 0, work_first, dict(acts_in=acts_in, out_grad=out_grad), {},
        gathers=dict(rows_mix=0, rows_out=0), helpers=[few, load],
    )
    few = few.result
    first = Bag(rows_mix=got.rows_mix, mixer=load.results[0], shared_w=load.results[1], acts_in=acts_in)
    second = Bag(rows_out=got.rows_out, out_grad=out_grad)
    for layer, k in enumerate((first, second)):
        x = dict(acts_in=acts_in) if layer == 0 else dict(x=second.x)
        load = Cargo(
            layer, dp, ffn_shard,
            {
                BEGIN: 1, 1: 1, 2: 3, 3: 3, SENT: 2, CHUNK: 1, CHUNK + 1: 1, CHUNK + 2: 1, CHUNK + 3: 1,
                SPREAD: 1, GIVEN: 2,
            },
        )
        k.add(
            run(
                f"mixer{layer}", 1 + layer, functools.partial(work_mid, layer),
                dict(x, few=few, rows_mix=k.rows_mix, mixer=k.mixer, shared_w=k.shared_w),
                dict(core_keeps, residual=block32, rest=((depth, 6 * LANES), B16)),
                need=dict({n: SENT for n in x}, rows_mix=1),
                done=dict(rest=0, proj=1, step=1, y=2, states=2, lows=3, lse=3, residual=CHUNK + 3),
                scratch=dict(state=pltpu.VMEM((NS, width), F32)),
                phases=functools.partial(core_fwd_phases, cols, members, layer, q_heads),
                part_width=depth, gathers=dict(rows_ffn=0), helpers=[load],
            )
        )
        k.gates = load.result
        if layer == 0:
            load = Cargo(
                1, dp, mixer_shard,
                {
                    BEGIN: 1, 0: 1, 1: 1, SENT: 3, CHUNK: 1, CHUNK + 1: 1, CHUNK + 2: 1, CHUNK + 3: 2, SPREAD: 1,
                    GIVEN: 3,
                },
                members, at_row.shared,
            )
            got = run(
                "turn", 3, work_turn,
                dict(residual=k.residual, few=few, rows_ffn=k.rows_ffn, gates=k.gates),
                dict(ffn_keeps, x=block16),
                need=dict(residual=SENT, few=SENT), done=dict(gu=0, hidden=0, x=CHUNK + 3),
                phases=ffn_fwd_phases, part_width=depth, gathers=dict(rows_mix=0), helpers=[load],
            )
            k.gu, k.hidden = got.gu, got.hidden
            second.rows_mix, second.x = got.rows_mix, got.x
            second.mixer, second.shared_w = load.results

    acts = Place(
        lambda r: (r.raw.x, r.last), (rows, depth), 1,
        {BEGIN: 1, CHUNK: 1, CHUNK + 1: 1, CHUNK + 2: 1, CHUNK + 3: 1},
    )
    second.add(
        run(
            "ffn1", 4, functools.partial(work_back_ffn, 1),
            dict(
                out_grad=out_grad, residual=second.residual, few=few, rows_ffn=second.rows_ffn,
                rows_out=second.rows_out, gates=second.gates, x=second.x,
            ),
            dict(gain_ffn=gain_row, g_gu=gu_spec, g_down=down_spec, d_residual=block32),
            need=dict(out_grad=SENT, residual=SENT, few=SENT, x=None, rows_out=2),
            done=dict(gain_ffn=3, g_gu=SENT, d_residual=CHUNK + 3, g_down=SPREAD),
            scratch=dict(
                last=pltpu.VMEM(*block16),
                **{n: pltpu.VMEM(*spec) for n, spec in ffn_keeps.items()},
                dgu=pltpu.VMEM((length, 2 * units), B16),
            ),
            phases=lambda r: ffn_fwd_phases(r, depth) + ffn_bwd_phases(r),
            fills=fills_ffn, part_width=2 * depth, gathers=dict(rows_back=0), helpers=[acts],
        )
    )

    core_scratch = dict(
        dproj=pltpu.VMEM((length, cols.total), B16),
        heads=pltpu.VMEM((8, LANES), F32),
        dcore=pltpu.VMEM((length, low_units), B16),
        grad_state=pltpu.VMEM((NS, width), F32),
        skip_sum=pltpu.VMEM((STEP, width), F32),
        dk_sum=pltpu.VMEM((length, LANES), F32),
        dv_sum=pltpu.VMEM((length, LANES), F32),
        folded=pltpu.VMEM((length, wide), B16),
        gain_sum=pltpu.VMEM((8, depth), F32),
        staged=pltpu.VMEM((depth, wide), F32),
    )

    def core_inputs(k):
        return dict(
            few=few, rows_mix=k.rows_mix, mixer=k.mixer, rows_back=k.rows_back, d_residual=k.d_residual,
            gain_ffn=k.gain_ffn, proj=k.proj, step=k.step, y=k.y, lows=k.lows, states=k.states,
            lse=k.lse, rest=k.rest,
        )

    core_need = dict(
        lows=1, proj=2, lse=2, few=3, step=3, y=3, states=3, rows_mix=4, gain_ffn=5, g_gu=2, g_down=1,
        d_residual=SENT, x=SENT, acts_in=SENT,
    )

    def core_phases(layer, r):
        return core_bwd_phases(cols, layer, members, (q_heads, heads), r)

    def from_input(pick):
        return lambda r: (pick(r.raw), pick(r))

    def from_kernel(pick):
        return lambda r: (pick(r), pick(r))

    take_gu, take_down = (lambda r: r.g_gu), (lambda r: r.g_down)
    take_cat, take_out, take_shared = (lambda r: r.g_cat), (lambda r: r.g_out), (lambda r: r.shared)

    def back_phases(layer, r):
        into, attend, scan, back, shared = core_phases(layer, r)
        steps = [into, lambda: fill_out(r), attend, scan]
        return steps + ([back, shared] if layer else [lambda: fill_cat(r), back, shared])

    hauls = [
        Haul(
            1, dp, [from_input(take_gu), from_input(take_down)], [gu_spec, down_spec],
            {BEGIN: 1, 2: 1, 3: 1, 4: 1, SENT: 1, CHUNK + 2: 1},
        ),
        Straight(1, dp, from_kernel(take_out), out_spec, {1: 1, CHUNK + 2: 1}),
        Haul(
            1, dp, [from_kernel(take_cat)], [cat_spec], {SENT: 1, SPREAD: 1, GIVEN: 1}, line=False
        ),
    ]
    inner = dict(g_cat=pltpu.VMEM(*cat_spec), g_out=pltpu.VMEM(*out_spec))
    got = run(
        "back1", 5, functools.partial(work_back_mix, 1),
        dict(core_inputs(second), x=second.x, g_gu=second.g_gu, g_down=second.g_down),
        dict(x_grad=block16, shared=shared_spec),
        need=dict(core_need, rest=4),
        done=dict(x_grad=CHUNK + 3, shared=CHUNK + 3),
        scratch=dict(core_scratch, **inner), phases=functools.partial(back_phases, 1), fills=[fill_cat],
        part_width=depth + wide, gathers=dict(rows_out=0), helpers=hauls,
    )
    second.add(got)
    cat_sums = hauls[2].result
    second.sums = hauls[0].results + hauls[1].results

    hauls = [
        Haul(
            1, dp, [from_input(lambda r: r.cat_sums)], [cat_spec], {BEGIN: 1, CHUNK + 3: 1}, swap=False
        ),
        Haul(
            1, dp, [from_input(take_shared)], [shared_spec], {BEGIN: 1, 1: 1, SENT: 2, CHUNK + 1: 1, GIVEN: 1}
        ),
        Haul(
            0, dp, [from_kernel(take_gu)], [gu_spec], {SENT: 1, CHUNK + 3: 1, SPREAD: 1, GIVEN: 1},
            line=False,
        ),
    ]
    got = run(
        "ffn0", 6, functools.partial(work_back_ffn, 0),
        dict(
            cotangent=second.x_grad, residual=first.residual, few=few, rows_ffn=first.rows_ffn,
            rows_out=second.rows_out, gates=first.gates, gu=first.gu, hidden=first.hidden,
            cat_sums=cat_sums, shared=second.shared,
        ),
        dict(gain_ffn=gain_row, g_down=down_spec, d_residual=block32),
        need=dict(
            cotangent=SENT, residual=SENT, few=SENT, rows_ffn=1, hidden=SENT, cat_sums=SENT, shared=1
        ),
        done=dict(gain_ffn=1, d_residual=CHUNK + 3, g_down=SPREAD),
        scratch=dict(dgu=pltpu.VMEM((length, 2 * units), B16), g_gu=pltpu.VMEM(*gu_spec)),
        phases=ffn_bwd_phases, fills=fills_ffn, part_width=depth, gathers=dict(rows_back=0),
        helpers=hauls,
    )
    gu_sums = hauls[2].result
    second.sums += hauls[0].results + hauls[1].results
    first.add(got)

    hauls = [
        Haul(0, dp, [from_input(lambda r: r.gu_sums)], [gu_spec], {BEGIN: 1, 3: 1}, swap=False),
        Haul(
            0, dp, [from_input(take_down)], [down_spec], {BEGIN: 1, 1: 1, 2: 2, 3: 1, 5: 1}
        ),
        Haul(0, dp, [from_kernel(take_out)], [out_spec], {1: 1, 3: 2, 4: 2, SENT: 1}),
        Haul(
            0, dp, [from_kernel(take_cat)], [cat_spec],
            {4: 1, 6: 1, SENT: 1, CHUNK: 1, CHUNK + 1: 1},
        ),
        Straight(0, dp, from_kernel(take_shared), shared_spec, {CHUNK + 3: 1}),
    ]
    x_grads = Place(
        lambda r: (r.x_grad, r.raw.x_grad1), (rows, depth), 0,
        {4: 1, CHUNK: 1, CHUNK + 1: 1, CHUNK + 2: 1, CHUNK + 3: 1},
    )
    run(
        "back0", 7, functools.partial(work_back_mix, 0),
        dict(core_inputs(first), acts_in=acts_in, x_grad1=second.x_grad, gu_sums=gu_sums, g_down=first.g_down),
        {},
        need=dict(core_need, x_grad1=None, gu_sums=3, rest=5, gain_ffn=6),
        scratch=dict(
            core_scratch, **inner, x_grad=pltpu.VMEM(*block16), shared=pltpu.VMEM(*shared_spec)
        ),
        phases=functools.partial(back_phases, 0), part_width=depth + wide, helpers=hauls + [x_grads],
    )
    first.sums = [h.result for h in hauls]
    order = [0, 1, 3, 2, 4]
    g_gates, g_down, g_cat, g_out, g_shared = [
        jnp.where(section == 0, first.sums[i], second.sums[j]).astype(F32).reshape(
            (-1,) + first.sums[i].shape[2:]
        )
        for i, j in zip(order, (0, 1, 3, 2, 4))
    ]
    g_mixer = jnp.stack([g_cat[:, :real], g_cat[:, width : width + real]], axis=1)
    table = 2 * NS + 2 * KVH * HD
    g_gains = g_shared[:, table + GAINS_AT : table + GAINS_AT + 2].T
    g_heads = g_shared[:3, table + HEADS_AT : table + HEADS_AT + heads]
    return (
        acts.result[None],
        x_grads.result[None],
        g_gains[None],
        g_mixer[None],
        g_cat[None, :, cols.q : cols.q + q_real],
        g_shared[None, :, :table],
        g_shared[None, :, table : table + HM],
        g_heads[None],
        g_out[None, :real],
        g_out[None, width : width + q_real],
        g_gates.reshape(1, piece, 2, units),
        g_down[None],
    )


def solution(mesh):
    rows = P(DP, TENSOR, None)
    by_dp, by_tensor, by_both = P(PIPE, DP), P(PIPE, TENSOR), P(PIPE, DP, TENSOR)
    wide, tall, whole = P(PIPE, DP, None, TENSOR), P(PIPE, TENSOR, DP), P(PIPE, DP, None)
    joint = P(PIPE, (DP, TENSOR), None)
    return jax.shard_map(
        on_device,
        mesh=mesh,
        in_specs=(
            rows, rows, by_dp, wide, by_both, whole, whole, by_tensor, by_tensor, by_tensor, tall, tall,
            by_dp, wide, tall,
        ),
        out_specs=(
            P(PIPE, DP, TENSOR, None), P(PIPE, DP, TENSOR, None), P(PIPE, None, (DP, TENSOR)),
            wide, by_both, joint, joint, P(PIPE, None, TENSOR), tall, tall, wide, tall,
        ),
        check_vma=False,
    )
```

profile of v0, /device:TPU:8, one launch (start us, length us, event | category | flops | bytes accessed | tf_op | source)
XLA Modules:
  0.0 514.2 jit_solution(6685823902196757441)
XLA Ops:
  0.7 0.7 pad.17
  1.4 0.7 pad.18
  2.0 0.7 pad.19
  2.7 0.7 dynamic-slice_bitcast_fusion.1
  3.4 1.9 concatenate.25.refs_2_
  5.4 0.8 slice_bitcast_fusion.8
  6.2 1.9 fusion.8
  8.3 0.7 fusion.7
  9.2 52.4 %first.1 = (bf16[1024,1024]{1,0:T(8,128)(2,1)}, bf16[1024,1024]{1,0:T(8,128)(2,1)}, f32[2,4,16,256]{3,2,1,0:T(8,128)}, bf16[4,1536,256]{2,1,0:T(8,128)(2,1)}, bf16[4,4,128,256]{3,2,1,0:T(8,128)(2,1)}) custom-call(bf16[2,256,1024]{2,1,0:T(8,128)(2,1)} %refs_13_.1, bf16[2,256,1024]{2,1,0:T(8,128)(2,1)} %refs_0_.5, f32[16,256]{1,0:T(8,128)} %concatenate.25.refs_2_, ...), custom_call_target="tpu_custom_call" | custom-call | flops 20000000000 | bytes 50000000 | tf_op jit(solution)/shard_map/first/pallas_call | solution.py:1394
  61.6 55.5 %mixer0.1 = (bf16[1024,1408]{1,0:T(8,128)(2,1)}, f32[1024,128]{1,0:T(8,128)}, bf16[1024,384]{1,0:T(8,128)(2,1)}, bf16[1024,512]{1,0:T(8,128)(2,1)}, bf16[8,128,3...) custom-call(bf16[2,256,1024]{2,1,0:T(8,128)(2,1)} %refs_13_.1, ...), custom_call_target="tpu_custom_call" | custom-call | flops 20000000000 | bytes 50000000 | tf_op jit(solution)/shard_map/mixer0/pallas_call | solution.py:1394
  117.1 51.9 %turn.1 = (bf16[1024,1024]{1,0:T(8,128)(2,1)}, bf16[1024,512]{1,0:T(8,128)(2,1)}, bf16[256,1024]{1,0:T(8,128)(2,1)}, bf16[1024,1024]{1,0:T(8,128)(2,1)}, bf16[4,...) custom-call(f32[256,1024]{1,0:T(8,128)} %get-tuple-element.73.refs_0_.refs_1_, ...), custom_call_target="tpu_custom_call" | custom-call | flops 20000000000 | bytes 50000000 | tf_op jit(solution)/shard_map/turn/pallas_call | solution.py:1394
  169.0 53.7 %mixer1.1 = (bf16[1024,1408]{1,0:T(8,128)(2,1)}, f32[1024,128]{1,0:T(8,128)}, bf16[1024,384]{1,0:T(8,128)(2,1)}, bf16[1024,512]{1,0:T(8,128)(2,1)}, bf16[8,128,3...) custom-call(bf16[256,1024]{1,0:T(8,128)(2,1)} %get-tuple-element.76., ...), custom_call_target="tpu_custom_call" | custom-call | flops 20000000000 | bytes 50000000 | tf_op jit(solution)/shard_map/mixer1/pallas_call | solution.py:1394
  222.8 55.2 %ffn1.1 = (f32[8,1024]{1,0:T(8,128)}, bf16[2,4,128,1024]{3,2,1,0:T(8,128)(2,1)}, bf16[2,4,256,256]{3,2,1,0:T(8,128)(2,1)}, f32[256,1024]{1,0:T(8,128)}, bf16[102...) custom-call(bf16[2,256,1024]{2,1,0:T(8,128)(2,1)} %refs_0_.5, f32[256,1024]{1,0:T(8,128)} %get-tuple-element.80.refs_1_, ...), custom_call_target="tpu_custom_call" | custom-call | flops 20000000000 | bytes 50000000 | tf_op jit(solution)/shard_map/ffn1/pallas_call | solution.py:1394
  278.0 82.0 %back1.1 = (bf16[256,1024]{1,0:T(8,128)(2,1)}, f32[2,4,32,640]{3,2,1,0:T(8,128)}, bf16[1024,1024]{1,0:T(8,128)(2,1)}, bf16[2,128,1024]{2,1,0:T(8,128)(2,1)}, bf1...) custom-call(f32[2,4,16,256]{3,2,1,0:T(8,128)} %get-tuple-element.69.refs_1_.refs_2_.refs_0_, ...), custom_call_target="tpu_custom_call" | custom-call | flops 20000000000 | bytes 50000000 | tf_op jit(solution)/shard_map/back1/pallas_call | solution.py:1394
  360.0 45.0 %ffn0.1 = (f32[8,1024]{1,0:T(8,128)}, bf16[2,4,256,256]{3,2,1,0:T(8,128)(2,1)}, f32[256,1024]{1,0:T(8,128)}, bf16[1024,1024]{1,0:T(8,128)(2,1)}, bf16[2,128,896]...) custom-call(bf16[256,1024]{1,0:T(8,128)(2,1)} %get-tuple-element.97.refs_0_.refs_14_, ...), custom_call_target="tpu_custom_call" | custom-call | flops 20000000000 | bytes 50000000 | tf_op jit(solution)/shard_map/ffn0/pallas_call | solution.py:1394
  405.0 94.1 %back0.1 = (bf16[2,128,1024]{2,1,0:T(8,128)(2,1)}, bf16[2,256,256]{2,1,0:T(8,128)(2,1)}, bf16[2,256,256]{2,1,0:T(8,128)(2,1)}, bf16[2,128,896]{2,1,0:T(8,128)(2,...) custom-call(f32[2,4,16,256]{3,2,1,0:T(8,128)} %get-tuple-element.69.refs_1_.refs_2_.refs_0_, ...), custom_call_target="tpu_custom_call" | custom-call | flops 20000000000 | bytes 50000000 | tf_op jit(solution)/shard_map/back0/pallas_call | solution.py:1394
  499.2 1.1 broadcast_select_fusion.1
  500.3 1.0 broadcast_select_fusion.2
  501.3 1.1 broadcast_select_fusion
  502.5 1.9 reshape.54
  504.4 0.6 copy.45
  505.0 0.7 copy.52
  505.8 0.7 slice_bitcast_fusion.4
  506.4 0.6 copy.42
  507.1 0.7 slice_bitcast_fusion.3
  507.8 0.8 slice_bitcast_fusion
  508.6 0.8 bitcast_convert_fusion.1
  509.4 0.1 bitcast_convert_fusion
  509.5 0.7 slice_bitcast_fusion.5
  510.3 1.5 copy.44
  511.8 1.0 copy.79
  512.8 1.0 copy.80
  (59 shorter events, 0.8 us)
Async XLA Ops:
  0.6 4.7 copy-start
  5.3 2.9 copy-start.11
  6.2 2.1 copy-start.14
  6.2 2.1 copy-start.2
  8.2 1.0 copy-start.8
  8.3 0.9 copy-start.16
  9.2 52.4 %copy-start.15 = (bf16[1536,256]{1,0:T(8,128)(2,1)}, bf16[1536,256]{1,0:T(8,128)(2,1)S(1)}, u32[]{:S(2)}) copy-start(bf16[1536,256]{1,0:T(8,128)(2,1)S(1)} %bitcast_dynamic-update-slice_fusion.refs_5_) | copy-start | bytes 2359300
  405.0 94.2 %copy-start.10 = (bf16[2,256,256]{2,1,0:T(8,128)(2,1)S(1)}, bf16[2,256,256]{2,1,0:T(8,128)(2,1)}, u32[]{:S(2)}) copy-start(bf16[2,256,256]{2,1,0:T(8,128)(2,1)} %get-tuple-element.125) | copy-start | bytes 786436
  405.0 95.3 %copy-start.9 = (bf16[2,256,256]{2,1,0:T(8,128)(2,1)S(1)}, bf16[2,256,256]{2,1,0:T(8,128)(2,1)}, u32[]{:S(2)}) copy-start(bf16[2,256,256]{2,1,0:T(8,128)(2,1)} %get-tuple-element.121) | copy-start | bytes 786436
  405.0 96.3 %copy-start.7 = (bf16[2,128,896]{2,1,0:T(8,128)(2,1)S(1)}, bf16[2,128,896]{2,1,0:T(8,128)(2,1)}, u32[]{:S(2)}) copy-start(bf16[2,128,896]{2,1,0:T(8,128)(2,1)} %get-tuple-element.119) | copy-start | bytes 1376260
  499.1 3.2 copy-start.12
  499.1 3.2 copy-start.13
  499.1 3.3 copy-start.5
  499.2 3.3 copy-start.6
  510.1 1.6 copy-start.3
  510.3 2.5 copy-start.4
  510.3 3.4 copy-start.1
where the time goes:
time: 523 us; the launch traced here: 514 us
  Pallas kernels  490 us (94%)
  local copies, waits for them, and re-layouts  18.5 us (4%)
    pallas_call x8, Pallas kernels, exchange(): pl.pallas_call(functools.partial(exchange_kernel, plan), out_shape=shapes...  490 us

commit v1 on v0

--- a/solution.py
+++ b/solution.py
@@ -141,43 +141,40 @@
     return total
 
 
-def multiply_out(lows_ref, weights_ref, first, part_ref, at=0):
+def multiply_out(lows_ref, weights_ref, first, part_ref, rows, at=0):
     ways, _, piece = weights_ref.shape
     last = first + lows_ref.shape[1]
-
-    def out_rows(i, _):
-        rows = pl.ds(pl.multiple_of(i * TILE, TILE), TILE)
-        block = lows_ref[rows, :]
-        for k in range(ways):
-            part_ref[rows, at + k * piece : at + (k + 1) * piece] = nn(
-                block, weights_ref[k, first:last, :]
-            ).astype(B16)
-        return 0
-
-    lax.fori_loop(0, lows_ref.shape[0] // TILE, out_rows, 0)
-
-
-def multiply_back(grad_ref, weights_ref, first, count, part_ref, rows_ref, gain_sum, rest=None):
+    block = lows_ref[rows, :]
+    for k in range(ways):
+        part_ref[rows, at + k * piece : at + (k + 1) * piece] = nn(
+            block, weights_ref[k, first:last, :]
+        ).astype(B16)
+
+
+def multiply_back(grad_ref, weights_ref, first, count, part_ref, rows, rows_ref, gain_sum, rest=None):
     ways, _, piece = weights_ref.shape
-    gain_sum[...] = jnp.zeros_like(gain_sum)
-
-    def out_rows(i, _):
-        rows = pl.ds(pl.multiple_of(i * TILE, TILE), TILE)
-        for d in range(ways):
-            to = slice(d * piece, (d + 1) * piece)
-            total = nt(grad_ref[rows, 0:piece], weights_ref[d, first : first + piece, :])
-            for c in range(1, count):
-                at = slice(first + c * piece, first + (c + 1) * piece)
-                total += nt(grad_ref[rows, c * piece : (c + 1) * piece], weights_ref[d, at, :])
-            if rest is not None:
-                total += nt(grad_ref[rows, count * piece :], rest[to, :])
-            part_ref[rows, to] = total.astype(B16)
-            gain_sum[0:1, to] += jnp.sum(
-                total * rows_ref[rows, to].astype(F32), axis=0, keepdims=True
-            )
-        return 0
-
-    lax.fori_loop(0, grad_ref.shape[0] // TILE, out_rows, 0)
+    for d in range(ways):
+        to = slice(d * piece, (d + 1) * piece)
+        total = nt(grad_ref[rows, 0:piece], weights_ref[d, first : first + piece, :])
+        for c in range(1, count):
+            at = slice(first + c * piece, first + (c + 1) * piece)
+            total += nt(grad_ref[rows, c * piece : (c + 1) * piece], weights_ref[d, at, :])
+        if rest is not None:
+            total += nt(grad_ref[rows, count * piece :], rest[to, :])
+        part_ref[rows, to] = total.astype(B16)
+        if gain_sum is not None:
+            gain_sum[0:1, to] += jnp.sum(total * rows_ref[rows, to].astype(F32), axis=0, keepdims=True)
+
+
+def by_blocks(order, rows, step):
+    def phase(group):
+        def run():
+            for member in group:
+                step(pl.ds(pl.multiple_of(member * rows, rows), rows), member)
+
+        return run
+
+    return [phase(group) for group in order]
 
 
 def skip_lanes(few_ref, layer, width):
@@ -190,7 +187,7 @@
     )[0:1, :]
 
 
-def core_fwd_phases(cols, members, layer, q_heads, r):
+def core_fwd_phases(cols, members, layer, q_heads, r, order):
     rows_ref, weights_ref, few_ref = r.rows_mix, r.mixer, r.few
     proj_ref, step_ref, y_ref, lows_ref = r.proj, r.step, r.y, r.lows
     states_ref, lse_ref, part_ref, state = r.states, r.lse, r.part, r.state
@@ -217,7 +214,7 @@
 
         lax.fori_loop(0, length // TILE, project, 0)
 
-    def scan_all():
+    def scan_part(low, high):
         ri, ci = iotas(STEP, STEP)
         lower = ri >= ci
         tril = lower.astype(F32)
@@ -225,7 +222,8 @@
         decay = jnp.exp(few_ref[layer, 0, 2:3, :LANES])
         bias = few_ref[layer, 0, 3:4, :LANES]
         skips = skip_lanes(few_ref, layer, width)
-        state[...] = jnp.zeros_like(state)
+        if low == 0:
+            state[...] = jnp.zeros_like(state)
 
         def scan_block(b, _):
             rows = pl.ds(pl.multiple_of(b * STEP, STEP), STEP)
@@ -268,57 +266,71 @@
             state[...] = states_in * jnp.concatenate(fades, axis=1) + fresh
             return 0
 
-        lax.fori_loop(0, length // STEP, scan_block, 0)
-
-    def attend_all():
+        lax.fori_loop(low, high, scan_block, 0)
+
+    def attend(i):
         rk, ck = iotas(TILE, 2 * TILE)
         diagonal = rk <= jnp.where(ck < TILE, ck, ck - TILE)
         q_low = iotas(TILE, LANES)[1] < HD
 
-        def attend(i, _):
-            rows = pl.ds(pl.multiple_of(i * TILE, TILE), TILE)
-            q2 = split_heads(proj_ref[rows, cols.q : cols.q + LANES], q_low)
-
-            def piece(j, carry, masked):
-                top, total, out = carry
-                keys = pl.ds(pl.multiple_of(j * TILE, TILE), TILE)
-                s = nt(proj_ref[keys, cols.k : cols.k + LANES], q2)
-                if masked:
-                    s = jnp.where(diagonal, s, -1e30)
-                new_top = jnp.maximum(top, jnp.max(s, axis=0, keepdims=True))
-                p = jnp.exp(s - new_top)
-                scale = jnp.exp(top - new_top)
-                total = total * scale + jnp.sum(p, axis=0, keepdims=True)
-                out = out * scale + tn(proj_ref[keys, cols.v : cols.v + LANES], p.astype(B16))
-                return new_top, total, out
-
-            carry = (
-                jnp.full((1, 2 * TILE), -1e30, F32),
-                jnp.zeros((1, 2 * TILE), F32),
-                jnp.zeros((LANES, 2 * TILE), F32),
-            )
-            carry = lax.fori_loop(0, i, lambda j, c: piece(j, c, False), carry)
-            top, total, out = piece(i, carry, True)
-            out = out / total
-            joined = jnp.concatenate([out[:HD, :TILE], out[HD:, TILE:]], axis=0)
-            lows_ref[rows, width : width + LANES] = joined.T.astype(B16)
-            lse_ref[i] = jnp.broadcast_to(top + jnp.log(total), (8, 2 * TILE))
-            return 0
-
-        lax.fori_loop(0, length // TILE, attend, 0)
-
-    def finish():
-        multiply_out(lows_ref, weights_ref, at_row.low, part_ref)
-
-    return [join_all, project_all, scan_all, attend_all, finish]
-
-
-def core_bwd_phases(cols, layer, members, q_heads, r):
+        rows = pl.ds(pl.multiple_of(i * TILE, TILE), TILE)
+        q2 = split_heads(proj_ref[rows, cols.q : cols.q + LANES], q_low)
+
+        def piece(j, carry, masked):
+            top, total, out = carry
+            keys = pl.ds(pl.multiple_of(j * TILE, TILE), TILE)
+            s = nt(proj_ref[keys, cols.k : cols.k + LANES], q2)
+            if masked:
+                s = jnp.where(diagonal, s, -1e30)
+            new_top = jnp.maximum(top, jnp.max(s, axis=0, keepdims=True))
+            p = jnp.exp(s - new_top)
+            scale = jnp.exp(top - new_top)
+            total = total * scale + jnp.sum(p, axis=0, keepdims=True)
+            out = out * scale + tn(proj_ref[keys, cols.v : cols.v + LANES], p.astype(B16))
+            return new_top, total, out
+
+        carry = (
+            jnp.full((1, 2 * TILE), -1e30, F32),
+            jnp.zeros((1, 2 * TILE), F32),
+            jnp.zeros((LANES, 2 * TILE), F32),
+        )
+        carry = lax.fori_loop(0, i, lambda j, c: piece(j, c, False), carry)
+        top, total, out = piece(i, carry, True)
+        out = out / total
+        joined = jnp.concatenate([out[:HD, :TILE], out[HD:, TILE:]], axis=0)
+        lows_ref[rows, width : width + LANES] = joined.T.astype(B16)
+        lse_ref[i] = jnp.broadcast_to(top + jnp.log(total), (8, 2 * TILE))
+
+    rows = length // members
+    blocks, tiles = length // STEP, length // TILE
+    together = rows == TILE
+
+    def attend_all():
+        for i in range(tiles):
+            attend(i)
+
+    def finish(at, member):
+        if together:
+            attend(member)
+        multiply_out(lows_ref, weights_ref, at_row.low, part_ref, at)
+
+    phases = [
+        join_all,
+        project_all,
+        lambda: scan_part(0, blocks // 2),
+        lambda: scan_part(blocks // 2, blocks),
+    ]
+    if not together:
+        phases[3] = lambda: (scan_part(blocks // 2, blocks), attend_all())
+    return phases + by_blocks(order, rows, finish)
+
+
+def core_bwd_phases(cols, layer, members, q_heads, r, order):
     back_ref, weights_ref, few_ref, rows_ref = r.rows_back, r.mixer, r.few, r.rows_mix
     proj_ref, step_ref, y_ref, lows_ref = r.proj, r.step, r.y, r.lows
     states_ref, lse_ref, part_ref = r.states, r.lse, r.part
     dproj_ref, heads_ref, dcore, grad_state, skip_sum = r.dproj, r.heads, r.dcore, r.grad_state, r.skip_sum
-    dk_sum, dv_sum, folded, gain_sum, staged = r.dk_sum, r.dv_sum, r.folded, r.gain_sum, r.staged
+    dk_sum, dv_sum, folded, staged = r.dk_sum, r.dv_sum, r.folded, r.staged
     length = back_ref.shape[0]
     width = cols.width
     ways, _, piece = weights_ref.shape
@@ -497,9 +509,9 @@
         skip = jnp.sum(skip_sum[...], axis=0, keepdims=True)
         heads_ref[2:3, :] = exact(jnp.broadcast_to(skip, (8, width)), group.astype(F32))[0:1, :]
 
-    def back_all():
+    def back(at, member):
         multiply_back(
-            dproj_ref, weights_ref, at_row.inner, cols.q // piece, part_ref, rows_ref, gain_sum, r.rest
+            dproj_ref, weights_ref, at_row.inner, cols.q // piece, part_ref, at, rows_ref, None, r.rest
         )
 
     def shared_all():
@@ -538,10 +550,12 @@
         for k in range(ways):
             at = slice(k * piece, (k + 1) * piece)
             grad = tn(rows_ref[:, at], folded[...])
-            columns = []
-            for row, sums in ((0, gain_sum), (1, r.gain_ffn)):
-                gain = few_ref[layer, k, row : row + 1, :]
-                columns.append(jnp.broadcast_to(sums[0:1, at] / gain, (LANES, piece)).T)
+            raw = nn(r.rest[at, LANES:], fold)
+            twice = (iotas(piece, wide)[1] >= 2 * LANES) & (iotas(piece, wide)[1] < 4 * LANES)
+            own = jnp.sum(grad * jnp.where(twice, 0.5 * raw, raw), axis=1, keepdims=True)
+            gains = [jnp.broadcast_to(few_ref[layer, k, i : i + 1, :], (LANES, piece)).T for i in (0, 1)]
+            from_ffn = jnp.broadcast_to(r.gain_ffn[0:1, at], (LANES, piece)).T
+            columns = [(own + r.gain_column[at, 0:1]) / gains[0], from_ffn / gains[1]]
             last = grad[:, wide - LANES :]
             last = jnp.where(lane == GAINS_AT, columns[0], last)
             last = jnp.where(lane == GAINS_AT + 1, columns[1], last)
@@ -553,75 +567,72 @@
                     staged[to : to + half, wide - LANES :] = last[rows, :]
             to = pl.multiple_of(member * (depth // members) + k * half, 8)
             staged[pl.ds(to, 8), wide - LANES :] += shifted
-        part_ref[:, depth:] = staged[...].astype(B16)
-
-    return [into_all, attend_all, scan_all, back_all, shared_all]
-
-
-def ffn_fwd_phases(r, at=0):
+        r.extra[...] = staged[...].astype(B16)
+
+    return [into_all, attend_all, scan_all, shared_all] + by_blocks(order, length // members, back)
+
+
+def ffn_forward(r, rows, at=0):
     rows_ref, weights_ref, gu_ref, hidden_ref = r.rows_ffn, r.gates, r.gu, r.hidden
     units = hidden_ref.shape[1]
     piece = weights_ref.shape[2]
     count = units // piece
-
-    def up(i, _):
-        rows = pl.ds(pl.multiple_of(i * TILE, TILE), TILE)
-        for c in range(count):
-            at = slice(c * piece, (c + 1) * piece)
-            g = blocks_nn(rows_ref, rows, weights_ref, c)
-            v = blocks_nn(rows_ref, rows, weights_ref, c + count)
-            gu_ref[rows, at] = g.astype(B16)
-            gu_ref[rows, units + c * piece : units + (c + 1) * piece] = v.astype(B16)
-            hidden_ref[rows, at] = (g * sigmoid(g) * v).astype(B16)
-        return 0
-
-    def up_all():
-        lax.fori_loop(0, rows_ref.shape[0] // TILE, up, 0)
-
-    def down_all():
-        multiply_out(hidden_ref, weights_ref, 2 * units, r.part, at)
-
-    return [up_all, down_all]
-
-
-def ffn_bwd_phases(r):
+    for c in range(count):
+        to = slice(c * piece, (c + 1) * piece)
+        g = blocks_nn(rows_ref, rows, weights_ref, c)
+        v = blocks_nn(rows_ref, rows, weights_ref, c + count)
+        gu_ref[rows, to] = g.astype(B16)
+        gu_ref[rows, units + c * piece : units + (c + 1) * piece] = v.astype(B16)
+        hidden_ref[rows, to] = (g * sigmoid(g) * v).astype(B16)
+    multiply_out(hidden_ref, weights_ref, 2 * units, r.part, rows, at)
+
+
+def ffn_backward(r, rows):
     out_ref, weights_ref, gu_ref, dgu_ref = r.rows_out, r.gates, r.gu, r.dgu
     ways, _, piece = weights_ref.shape
     units = gu_ref.shape[1] // 2
     down_rows = slice(2 * units, 3 * units)
-
-    def down(i, _):
-        rows = pl.ds(pl.multiple_of(i * TILE, TILE), TILE)
-        dh = nt(out_ref[rows, 0:piece], weights_ref[0, down_rows, :])
-        for k in range(1, ways):
-            dh += nt(out_ref[rows, k * piece : (k + 1) * piece], weights_ref[k, down_rows, :])
-        g = gu_ref[rows, :units].astype(F32)
-        v = gu_ref[rows, units:].astype(F32)
-        sg = sigmoid(g)
-        dgu_ref[rows, :units] = (dh * v * sg * (1.0 + g * (1.0 - sg))).astype(B16)
-        dgu_ref[rows, units:] = (dh * g * sg).astype(B16)
-        return 0
-
-    def down_all():
-        lax.fori_loop(0, out_ref.shape[0] // TILE, down, 0)
-
-    def back_all():
-        multiply_back(
-            dgu_ref, weights_ref, 0, 2 * units // piece, r.part, r.rows_ffn, r.gain_ffn
-        )
-
-    return [down_all, back_all]
-
-
-def grad_columns(rows_ref, grad_ref, out_ref):
+    dh = nt(out_ref[rows, 0:piece], weights_ref[0, down_rows, :])
+    for k in range(1, ways):
+        dh += nt(out_ref[rows, k * piece : (k + 1) * piece], weights_ref[k, down_rows, :])
+    g = gu_ref[rows, :units].astype(F32)
+    v = gu_ref[rows, units:].astype(F32)
+    sg = sigmoid(g)
+    dgu_ref[rows, :units] = (dh * v * sg * (1.0 + g * (1.0 - sg))).astype(B16)
+    dgu_ref[rows, units:] = (dh * g * sg).astype(B16)
+    multiply_back(
+        dgu_ref, weights_ref, 0, 2 * units // piece, r.part, rows, r.rows_ffn, r.gain_ffn
+    )
+
+
+def grad_columns(rows_ref, grad_ref, out_ref, step=512, weigh=None):
     _, ways, half, width = out_ref.shape
     for k in range(ways):
         block = rows_ref[:, 2 * half * k : 2 * half * (k + 1)]
-        for first in range(0, width, 512):
-            last = min(first + 512, width)
-            value = tn(block, grad_ref[:, first:last]).astype(B16)
+        for first in range(0, width, step):
+            last = min(first + step, width)
+            value = tn(block, grad_ref[:, first:last])
+            if weigh:
+                weigh(k, first, last, value)
+            value = value.astype(B16)
             out_ref[0, k, :, first:last] = value[:half, :]
             out_ref[1, k, :, first:last] = value[half:, :]
+
+
+def mixer_columns(cols, members, r):
+    _, _, piece = r.mixer.shape
+    inner = MixerRows(cols, members).inner
+    r.gain_column[...] = jnp.zeros_like(r.gain_column)
+
+    def weigh(k, first, last, value):
+        rows = slice(k * piece, (k + 1) * piece)
+        if first < cols.q:
+            weight = r.mixer[k, inner + first : inner + last, :]
+        else:
+            weight = r.rest[rows, :LANES]
+        r.gain_column[rows, 0:1] += jnp.sum(value * weight.astype(F32), axis=1, keepdims=True)
+
+    grad_columns(r.rows_mix, r.dproj, r.g_cat, piece, weigh)
 
 
 def grad_rows(lows_ref, back_ref, out_ref):
@@ -635,8 +646,9 @@
 DMA = pltpu.SemaphoreType.DMA
 MESH = pl.DeviceIdType.MESH
 PIPE, DP, TENSOR = "pipe", "dp", "tensor"
-
-BEGIN, SENT, CHUNK, SPREAD, GIVEN, END = -1, 20, 30, 40, 50, 60
+PART, SHARED = "part", "extra"
+
+BEGIN, SENT, EXTRA, CHUNK, SPREAD, GIVEN, END = -1, 20, 25, 30, 40, 50, 60
 
 
 class Bag:
@@ -1152,60 +1164,136 @@
         return [early] + [functools.partial(hand, self.late, c) for c in range(self.PIECES)] + [finish]
 
 
+class Members:
+    def __init__(self, count):
+        self.pairs = count // 2
+        self.me = lax.axis_index(TENSOR)
+        self.mine, self.side = self.me // 2, self.me % 2
+        self.sibling = 2 * self.mine + 1 - self.side
+
+    def far(self, k):
+        return 2 * ((self.mine + k) % self.pairs) + self.side
+
+    def across(self, k):
+        return 2 * ((self.mine + k) % self.pairs) + 1 - self.side
+
+    def order(self):
+        others = range(1, self.pairs)
+        return [[self.across(k) for k in others], [self.far(k) for k in others], [self.sibling], [self.me]]
+
+
+def member_copy(source, target, send, receive, member):
+    return remote(source, target, send, receive, {TENSOR: member})
+
+
+class Scatter:
+    @staticmethod
+    def scratch(members, rows, width, pieces):
+        pairs = members // 2
+        others = max(pairs - 1, 1)
+        return [
+            pltpu.VMEM((pairs, rows, width), B16),
+            pltpu.VMEM((others, rows, width), B16),
+            pltpu.VMEM((others, rows, width), B16),
+            DMA((pairs, pieces)), DMA((pairs, pieces)), DMA((others, pieces)), DMA((others, pieces)),
+        ]
+
+    def __init__(self, part_ref, members, rows, pieces, scratch):
+        self.part, self.at, self.rows, self.pieces = part_ref, members, rows, pieces
+        self.size = rows // pieces
+        self.pair_in, self.far_out, self.far_in = scratch[:3]
+        self.pair_send, self.pair_recv, self.far_send, self.far_recv = scratch[3:]
+
+    def rows_of(self, member, c):
+        return pl.ds(pl.multiple_of(member * self.rows + c * self.size, self.size), self.size)
+
+    def chunk(self, c):
+        return pl.ds(c * self.size, self.size)
+
+    def to_pair(self, k, c):
+        member = self.at.across(k) if k else self.at.sibling
+        return member_copy(
+            self.part.at[self.rows_of(member, c), :], self.pair_in.at[k, self.chunk(c), :],
+            self.pair_send.at[k, c], self.pair_recv.at[k, c], self.at.sibling,
+        )
+
+    def to_far(self, k, c, slot):
+        return member_copy(
+            self.far_out.at[k - 1, self.chunk(c), :], self.far_in.at[slot - 1, self.chunk(c), :],
+            self.far_send.at[k - 1, c], self.far_recv.at[slot - 1, c], self.at.far(k),
+        )
+
+    def send_across(self):
+        for c in range(self.pieces):
+            for k in range(1, self.at.pairs):
+                self.to_pair(k, c).start()
+
+    def send_far(self):
+        for c in range(self.pieces):
+            for k in range(1, self.at.pairs):
+                self.to_pair(k, c).wait_recv()
+                total = self.part[self.rows_of(self.at.far(k), c), :].astype(F32)
+                total += self.pair_in[k, self.chunk(c), :].astype(F32)
+                self.far_out[k - 1, self.chunk(c), :] = total.astype(B16)
+                self.to_far(k, c, self.at.pairs - k).start()
+
+    def send_sibling(self):
+        for c in range(self.pieces):
+            self.to_pair(0, c).start()
+
+    def receive(self, c):
+        self.to_pair(0, c).wait_recv()
+        total = self.part[self.rows_of(self.at.me, c), :].astype(F32)
+        total += self.pair_in[0, self.chunk(c), :].astype(F32)
+        for k in range(1, self.at.pairs):
+            self.to_far(k, c, k).wait_recv()
+            total += self.far_in[k - 1, self.chunk(c), :].astype(F32)
+        return total
+
+    def finish(self):
+        for c in range(self.pieces):
+            for k in range(self.at.pairs):
+                self.to_pair(k, c).wait_send()
+                if k:
+                    self.to_far(k, c, self.at.pairs - k).wait_send()
+
+
 def exchange_kernel(plan, *refs):
     refs = list(refs)
 
     def take(count):
         return [refs.pop(0) for _ in range(count)]
 
-    r = Bag(raw=Bag())
-    held = {}
-    for name in plan.inputs:
-        held[name] = take(1)[0]
+    r = Bag()
+    held = {name: take(1)[0] for name in plan.inputs}
     r.raw = Bag(**held)
     helper_inputs = [take(len(h.inputs)) for h in plan.helpers]
     targets = {name: take(1)[0] for name in plan.outs}
     gathered = take(len(plan.gathers))
     helper_outs = [take(len(h.outs)) for h in plan.helpers]
     loaded = [name for name in plan.inputs if plan.need(name) is not None]
-    for name in loaded:
-        setattr(r, name, take(1)[0])
-    for name in plan.outs:
-        setattr(r, name, take(1)[0])
-    for name in plan.scratch:
+    for name in loaded + plan.outs + plan.scratch:
         setattr(r, name, take(1)[0])
     load_sem, store_sem = take(2)
-    if plan.scatter:
-        part_ref, pair_in, far_out, far_in, pair_send, pair_recv, far_send, far_recv = take(8)
-        r.part = part_ref
+    at = Members(plan.members)
+    pairs, pieces = at.pairs, plan.pieces
+    scatters = {}
+    for name, (_, count, _) in plan.scatters.items():
+        setattr(r, name, take(1)[0])
+        scatters[name] = Scatter(getattr(r, name), at, plan.rows, count, take(7))
     if plan.gathers:
         mine_refs = take(len(plan.gathers))
         give_send, give_recv, spread_send, spread_recv, keep_sem = take(5)
     helpers = []
     for h, inputs, outs in zip(plan.helpers, helper_inputs, helper_outs):
         helpers.append((h.bind(r, inputs, outs, take(len(h.scratch))), h.when))
-
-    members, pieces = plan.members, plan.pieces
-    pairs = members // 2
-    me = lax.axis_index(TENSOR)
-    mine, side = me // 2, me % 2
-    sibling = 2 * mine + 1 - side
     size = plan.rows // pieces
-
-    def far(k):
-        return 2 * ((mine + k) % pairs) + side
-
-    def across(k):
-        return 2 * ((mine + k) % pairs) + 1 - side
 
     def rows_of(member, c):
         return pl.ds(pl.multiple_of(member * plan.rows + c * size, size), size)
 
     def chunk(c):
         return pl.ds(c * size, size)
-
-    def copy(source, target, send, receive, member):
-        return remote(source, target, send, receive, {TENSOR: member})
 
     loads = {}
     for i, name in enumerate(sorted(loaded, key=plan.need)):
@@ -1228,9 +1316,13 @@
 
     def point(stage):
         for steps, when in helpers:
-            count = len(steps) if stage == END else when.get(stage, 0)
+            count = len(steps) - 1 if stage == END else when.get(stage, 0)
             for _ in range(min(count, len(steps))):
                 steps.pop(0)()
+        if stage == END:
+            for steps, _ in helpers:
+                while steps:
+                    steps.pop(0)()
         flush(stage)
 
     def run_fill(i):
@@ -1238,7 +1330,7 @@
             plan.fills[i](r)
 
     barrier = pltpu.get_barrier_semaphore()
-    greeted = [{TENSOR: sibling}] + [{TENSOR: far(k)} for k in range(1, pairs)]
+    greeted = [{TENSOR: at.sibling}] + [{TENSOR: at.far(k)} for k in range(1, pairs)]
     if helpers:
         greeted += cross_devices(plan.ways)
     for device in greeted:
@@ -1247,67 +1339,44 @@
 
     arrive(BEGIN)
     point(BEGIN)
-    for i, phase in enumerate(plan.phases(r) if plan.phases else []):
+    for i, phase in enumerate(plan.phases(r, at.order()) if plan.phases else []):
         arrive(i)
         phase()
+        for name, (_, _, ready) in plan.scatters.items():
+            for last, send in zip(
+                ready, (scatters[name].send_across, scatters[name].send_far, scatters[name].send_sibling)
+            ):
+                if last == i:
+                    send()
         point(i)
-
-    if plan.scatter:
-        to_pair = {}
-        for c in range(pieces):
-            for k in range(1, pairs):
-                to_pair[k, c] = copy(
-                    part_ref.at[rows_of(across(k), c), :], pair_in.at[k, chunk(c), :],
-                    pair_send.at[k, c], pair_recv.at[k, c], sibling,
-                )
-                to_pair[k, c].start()
-        for c in range(pieces):
-            to_pair[0, c] = copy(
-                part_ref.at[rows_of(sibling, c), :], pair_in.at[0, chunk(c), :],
-                pair_send.at[0, c], pair_recv.at[0, c], sibling,
-            )
-            to_pair[0, c].start()
-        to_far = {}
-        for c in range(pieces):
-            for k in range(1, pairs):
-                to_pair[k, c].wait_recv()
-                far_out[k - 1, chunk(c), :] = (
-                    part_ref[rows_of(far(k), c), :].astype(F32)
-                    + pair_in[k, chunk(c), :].astype(F32)
-                ).astype(B16)
-                to_far[k, c] = copy(
-                    far_out.at[k - 1, chunk(c), :], far_in.at[pairs - k - 1, chunk(c), :],
-                    far_send.at[k - 1, c], far_recv.at[pairs - k - 1, c], far(k),
-                )
-                to_far[k, c].start()
     arrive(SENT)
-    if plan.scatter:
+    if plan.phases:
         run_fill(0)
     point(SENT)
+    if plan.extra_work:
+        plan.extra_work(r, scatters)
+        point(EXTRA)
 
     given, spreads, keeps = {}, {}, []
     for c in range(pieces):
         total = None
-        if plan.scatter:
-            to_pair[0, c].wait_recv()
-            total = part_ref[rows_of(me, c), :].astype(F32) + pair_in[0, chunk(c), :].astype(F32)
-            for k in range(1, pairs):
-                copy(
-                    far_out.at[k - 1, chunk(c), :], far_in.at[k - 1, chunk(c), :],
-                    far_send.at[k - 1, c], far_recv.at[k - 1, c], far(k),
-                ).wait_recv()
-                total += far_in[k - 1, chunk(c), :].astype(F32)
+        if plan.phases:
+            for name in plan.scatters:
+                total = scatters[name].receive(c)
+                break
         results = plan.work(r, c, chunk(c), total)
         for g, rows_ref in enumerate(gathered):
             own = mine_refs[g].at[chunk(c), :]
-            there = rows_ref.at[rows_of(me, c), :]
+            there = rows_ref.at[rows_of(at.me, c), :]
             mine_refs[g][chunk(c), :] = results[g]
             for k in range(1, pairs):
-                spreads[g, k, c] = copy(
-                    own, there, spread_send.at[g, k - 1, c], spread_recv.at[g, pairs - k - 1, c], far(k)
+                spreads[g, k, c] = member_copy(
+                    own, there, spread_send.at[g, k - 1, c], spread_recv.at[g, pairs - k - 1, c], at.far(k)
                 )
                 spreads[g, k, c].start()
-            given[g, 0, c] = copy(own, there, give_send.at[g, 0, c], give_recv.at[g, 0, c], sibling)
+            given[g, 0, c] = member_copy(
+                own, there, give_send.at[g, 0, c], give_recv.at[g, 0, c], at.sibling
+            )
             given[g, 0, c].start()
             keeps.append(pltpu.make_async_copy(own, there, keep_sem.at[g, c]))
             keeps[-1].start()
@@ -1317,31 +1386,29 @@
     for g, rows_ref in enumerate(gathered):
         for c in range(pieces):
             for k in range(1, pairs):
-                block = rows_ref.at[rows_of(far(k), c), :]
-                copy(
-                    block, block, spread_send.at[g, k - 1, c], spread_recv.at[g, k - 1, c], far(k)
+                block = rows_ref.at[rows_of(at.far(k), c), :]
+                member_copy(
+                    block, block, spread_send.at[g, k - 1, c], spread_recv.at[g, k - 1, c], at.far(k)
                 ).wait_recv()
-                given[g, k, c] = copy(
-                    block, block, give_send.at[g, k, c], give_recv.at[g, k, c], sibling
+                given[g, k, c] = member_copy(
+                    block, block, give_send.at[g, k, c], give_recv.at[g, k, c], at.sibling
                 )
                 given[g, k, c].start()
     point(GIVEN)
     for g, rows_ref in enumerate(gathered):
         for c in range(pieces):
             for k in range(pairs):
-                block = rows_ref.at[rows_of(sibling if k == 0 else across(k), c), :]
-                copy(block, block, give_send.at[g, k, c], give_recv.at[g, k, c], sibling).wait_recv()
+                block = rows_ref.at[rows_of(at.across(k) if k else at.sibling, c), :]
+                member_copy(
+                    block, block, give_send.at[g, k, c], give_recv.at[g, k, c], at.sibling
+                ).wait_recv()
         for c in range(pieces):
             for k in range(pairs):
                 given[g, k, c].wait_send()
             for k in range(1, pairs):
                 spreads[g, k, c].wait_send()
-    if plan.scatter:
-        for c in range(pieces):
-            for k in range(pairs):
-                to_pair[k, c].wait_send()
-            for k in range(1, pairs):
-                to_far[k, c].wait_send()
+    for scatter in scatters.values():
+        scatter.finish()
     arrive(END)
     point(END)
     for store in stores + keeps:
@@ -1350,16 +1417,16 @@
 
 def exchange(
     name, number, members, ways, rows, depth, work, inputs, outs=None, need=None, done=None, scratch=None,
-    phases=None, fills=(), part_width=0, gathers=None, helpers=(), pieces=4,
+    phases=None, fills=(), scatters=None, extra_work=None, gathers=None, helpers=(), pieces=4,
 ):
     pairs = members // 2
     others = max(pairs - 1, 1)
     outs, scratch, need, done = outs or {}, scratch or {}, need or {}, done or {}
-    gathers = gathers or []
+    gathers, scatters = gathers or [], scatters or {}
     hbm, vmem = pl.BlockSpec(memory_space=pl.ANY), pl.BlockSpec(memory_space=pltpu.VMEM)
     plan = Bag(
         inputs=list(inputs), outs=list(outs), scratch=list(scratch), gathers=gathers, helpers=list(helpers),
-        members=members, ways=ways, rows=rows, pieces=pieces, scatter=bool(part_width),
+        members=members, ways=ways, rows=rows, pieces=pieces, scatters=scatters, extra_work=extra_work,
         phases=phases, fills=list(fills), work=work,
         need=lambda n: need.get(n, 0 if phases else BEGIN), done=lambda n: done.get(n, END),
     )
@@ -1367,14 +1434,9 @@
     staging += [pltpu.VMEM(*spec) for spec in outs.values()]
     staging += list(scratch.values())
     staging += [DMA((max(len(inputs), 1),)), DMA((max(len(outs), 1),))]
-    if part_width:
-        staging += [
-            pltpu.VMEM((members * rows, part_width), B16),
-            pltpu.VMEM((pairs, rows, part_width), B16),
-            pltpu.VMEM((others, rows, part_width), B16),
-            pltpu.VMEM((others, rows, part_width), B16),
-            DMA((pairs, pieces)), DMA((pairs, pieces)), DMA((others, pieces)), DMA((others, pieces)),
-        ]
+    for width, chunks, _ in scatters.values():
+        staging.append(pltpu.VMEM((members * rows, width), B16))
+        staging += Scatter.scratch(members, rows, width, chunks)
     count = len(gathers)
     if count:
         staging += [pltpu.VMEM((rows, depth), B16)] * count
@@ -1470,16 +1532,17 @@
 
 
 def work_back_mix(layer, r, c, at, total):
-    depth = r.d_residual.shape[1]
-    step = rms_back(layer_input(r, layer, at), gain_of(r, layer, 0), total[:, :depth])
+    step = rms_back(layer_input(r, layer, at), gain_of(r, layer, 0), total)
     grad = (r.d_residual[at, :] + step).astype(B16)
     r.x_grad[at, :] = grad
+    return (grad,)
+
+
+def work_shared(r, scatters):
+    total = scatters[SHARED].receive(0)
     _, ways, block, _ = r.shared.shape
-    blocks = total.shape[0] // block
-    for i in range(blocks):
-        j = c * blocks + i
-        r.shared[j // ways, j % ways] = total[i * block : (i + 1) * block, depth:]
-    return (grad,)
+    for j in range(2 * ways):
+        r.shared[j // ways, j % ways] = total[j * block : (j + 1) * block, :]
 
 
 def widen(block, axis, size):
@@ -1559,7 +1622,7 @@
         lambda r: grad_columns(r.rows_ffn, r.dgu, r.g_gu),
         lambda r: grad_rows(r.hidden, r.rows_out, r.g_down),
     ]
-    fill_cat = lambda r: grad_columns(r.rows_mix, r.dproj, r.g_cat)
+    fill_cat = lambda r: mixer_columns(cols, members, r)
     fill_out = lambda r: grad_rows(r.lows, r.rows_back, r.g_out)
 
     load = Cargo(
@@ -1580,8 +1643,8 @@
         load = Cargo(
             layer, dp, ffn_shard,
             {
-                BEGIN: 1, 1: 1, 2: 3, 3: 3, SENT: 2, CHUNK: 1, CHUNK + 1: 1, CHUNK + 2: 1, CHUNK + 3: 1,
-                SPREAD: 1, GIVEN: 2,
+                BEGIN: 1, 0: 1, 1: 1, 2: 1, 3: 2, 4: 1, 5: 1, 6: 1, 7: 2, SENT: 1, CHUNK: 1, CHUNK + 1: 1,
+                CHUNK + 2: 1, CHUNK + 3: 1, SPREAD: 2,
             },
         )
         k.add(
@@ -1590,10 +1653,10 @@
                 dict(x, few=few, rows_mix=k.rows_mix, mixer=k.mixer, shared_w=k.shared_w),
                 dict(core_keeps, residual=block32, rest=((depth, 6 * LANES), B16)),
                 need=dict({n: SENT for n in x}, rows_mix=1),
-                done=dict(rest=0, proj=1, step=1, y=2, states=2, lows=3, lse=3, residual=CHUNK + 3),
+                done=dict(rest=0, proj=1, step=1, y=3, states=3, lows=7, lse=7, residual=CHUNK + 3),
                 scratch=dict(state=pltpu.VMEM((NS, width), F32)),
                 phases=functools.partial(core_fwd_phases, cols, members, layer, q_heads),
-                part_width=depth, gathers=dict(rows_ffn=0), helpers=[load],
+                scatters={PART: (depth, 4, (4, 5, 6))}, gathers=dict(rows_ffn=0), helpers=[load],
             )
         )
         k.gates = load.result
@@ -1601,7 +1664,7 @@
             load = Cargo(
                 1, dp, mixer_shard,
                 {
-                    BEGIN: 1, 0: 1, 1: 1, SENT: 3, CHUNK: 1, CHUNK + 1: 1, CHUNK + 2: 1, CHUNK + 3: 2, SPREAD: 1,
+                    BEGIN: 1, 1: 1, 3: 1, SENT: 2, CHUNK: 2, CHUNK + 1: 1, CHUNK + 2: 1, CHUNK + 3: 1, SPREAD: 2,
                     GIVEN: 3,
                 },
                 members, at_row.shared,
@@ -1610,12 +1673,28 @@
                 "turn", 3, work_turn,
                 dict(residual=k.residual, few=few, rows_ffn=k.rows_ffn, gates=k.gates),
                 dict(ffn_keeps, x=block16),
-                need=dict(residual=SENT, few=SENT), done=dict(gu=0, hidden=0, x=CHUNK + 3),
-                phases=ffn_fwd_phases, part_width=depth, gathers=dict(rows_mix=0), helpers=[load],
+                need=dict(residual=SENT, few=SENT), done=dict(gu=3, hidden=3, x=CHUNK + 3),
+                phases=lambda r, order: by_blocks(order, rows, lambda at, m: ffn_forward(r, at)),
+                scatters={PART: (depth, 4, (0, 1, 2))}, gathers=dict(rows_mix=0), helpers=[load],
             )
             k.gu, k.hidden = got.gu, got.hidden
             second.rows_mix, second.x = got.rows_mix, got.x
             second.mixer, second.shared_w = load.results
+
+    def clear_gain(r):
+        r.gain_ffn[...] = jnp.zeros_like(r.gain_ffn)
+
+    def ffn_both(r, at, m):
+        ffn_forward(r, at, depth)
+        ffn_backward(r, at)
+
+    def ffn_both_phases(r, order):
+        clear_gain(r)
+        return by_blocks(order, rows, functools.partial(ffn_both, r))
+
+    def ffn_back_phases(r, order):
+        clear_gain(r)
+        return by_blocks(order, rows, lambda at, m: ffn_backward(r, at))
 
     acts = Place(
         lambda r: (r.raw.x, r.last), (rows, depth), 1,
@@ -1629,15 +1708,15 @@
                 rows_out=second.rows_out, gates=second.gates, x=second.x,
             ),
             dict(gain_ffn=gain_row, g_gu=gu_spec, g_down=down_spec, d_residual=block32),
-            need=dict(out_grad=SENT, residual=SENT, few=SENT, x=None, rows_out=2),
+            need=dict(out_grad=SENT, residual=SENT, few=SENT, x=None),
             done=dict(gain_ffn=3, g_gu=SENT, d_residual=CHUNK + 3, g_down=SPREAD),
             scratch=dict(
                 last=pltpu.VMEM(*block16),
                 **{n: pltpu.VMEM(*spec) for n, spec in ffn_keeps.items()},
                 dgu=pltpu.VMEM((length, 2 * units), B16),
             ),
-            phases=lambda r: ffn_fwd_phases(r, depth) + ffn_bwd_phases(r),
-            fills=fills_ffn, part_width=2 * depth, gathers=dict(rows_back=0), helpers=[acts],
+            phases=ffn_both_phases,
+            scatters={PART: (2 * depth, 4, (0, 1, 2))}, fills=fills_ffn, gathers=dict(rows_back=0), helpers=[acts],
         )
     )
 
@@ -1650,7 +1729,7 @@
         dk_sum=pltpu.VMEM((length, LANES), F32),
         dv_sum=pltpu.VMEM((length, LANES), F32),
         folded=pltpu.VMEM((length, wide), B16),
-        gain_sum=pltpu.VMEM((8, depth), F32),
+        gain_column=pltpu.VMEM((depth, LANES), F32),
         staged=pltpu.VMEM((depth, wide), F32),
     )
 
@@ -1662,12 +1741,12 @@
         )
 
     core_need = dict(
-        lows=1, proj=2, lse=2, few=3, step=3, y=3, states=3, rows_mix=4, gain_ffn=5, g_gu=2, g_down=1,
+        lows=1, proj=2, lse=2, few=3, step=3, y=3, states=3, rows_mix=4, rest=4, gain_ffn=5, g_gu=2, g_down=1,
         d_residual=SENT, x=SENT, acts_in=SENT,
     )
 
-    def core_phases(layer, r):
-        return core_bwd_phases(cols, layer, members, (q_heads, heads), r)
+    def core_phases(layer, r, order):
+        return core_bwd_phases(cols, layer, members, (q_heads, heads), r, order)
 
     def from_input(pick):
         return lambda r: (pick(r.raw), pick(r))
@@ -1678,19 +1757,19 @@
     take_gu, take_down = (lambda r: r.g_gu), (lambda r: r.g_down)
     take_cat, take_out, take_shared = (lambda r: r.g_cat), (lambda r: r.g_out), (lambda r: r.shared)
 
-    def back_phases(layer, r):
-        into, attend, scan, back, shared = core_phases(layer, r)
-        steps = [into, lambda: fill_out(r), attend, scan]
-        return steps + ([back, shared] if layer else [lambda: fill_cat(r), back, shared])
-
+    def back_phases(layer, r, order):
+        into, attend, scan, shared, *back = core_phases(layer, r, order)
+        return [into, lambda: fill_out(r), attend, scan, lambda: fill_cat(r), shared] + back
+
+    back_scatters = {PART: (depth, 4, (6, 7, 8)), SHARED: (wide, 1, (5, 6, 5))}
     hauls = [
         Haul(
             1, dp, [from_input(take_gu), from_input(take_down)], [gu_spec, down_spec],
-            {BEGIN: 1, 2: 1, 3: 1, 4: 1, SENT: 1, CHUNK + 2: 1},
+            {BEGIN: 1, 2: 1, 3: 1, 4: 1, SENT: 1, CHUNK + 3: 1},
         ),
-        Straight(1, dp, from_kernel(take_out), out_spec, {1: 1, CHUNK + 2: 1}),
+        Straight(1, dp, from_kernel(take_out), out_spec, {1: 1, SENT: 1}),
         Haul(
-            1, dp, [from_kernel(take_cat)], [cat_spec], {SENT: 1, SPREAD: 1, GIVEN: 1}, line=False
+            1, dp, [from_kernel(take_cat)], [cat_spec], {4: 1, CHUNK: 1, CHUNK + 1: 1, CHUNK + 2: 1, CHUNK + 3: 1}, line=False
         ),
     ]
     inner = dict(g_cat=pltpu.VMEM(*cat_spec), g_out=pltpu.VMEM(*out_spec))
@@ -1698,10 +1777,10 @@
         "back1", 5, functools.partial(work_back_mix, 1),
         dict(core_inputs(second), x=second.x, g_gu=second.g_gu, g_down=second.g_down),
         dict(x_grad=block16, shared=shared_spec),
-        need=dict(core_need, rest=4),
-        done=dict(x_grad=CHUNK + 3, shared=CHUNK + 3),
-        scratch=dict(core_scratch, **inner), phases=functools.partial(back_phases, 1), fills=[fill_cat],
-        part_width=depth + wide, gathers=dict(rows_out=0), helpers=hauls,
+        need=core_need,
+        done=dict(x_grad=CHUNK + 3, shared=EXTRA),
+        scratch=dict(core_scratch, **inner), phases=functools.partial(back_phases, 1),
+        scatters=back_scatters, extra_work=work_shared, gathers=dict(rows_out=0), helpers=hauls,
     )
     second.add(got)
     cat_sums = hauls[2].result
@@ -1712,7 +1791,7 @@
             1, dp, [from_input(lambda r: r.cat_sums)], [cat_spec], {BEGIN: 1, CHUNK + 3: 1}, swap=False
         ),
         Haul(
-            1, dp, [from_input(take_shared)], [shared_spec], {BEGIN: 1, 1: 1, SENT: 2, CHUNK + 1: 1, GIVEN: 1}
+            1, dp, [from_input(take_shared)], [shared_spec], {BEGIN: 1, 3: 1, SENT: 2, CHUNK + 1: 1, GIVEN: 1}
         ),
         Haul(
             0, dp, [from_kernel(take_gu)], [gu_spec], {SENT: 1, CHUNK + 3: 1, SPREAD: 1, GIVEN: 1},
@@ -1728,11 +1807,11 @@
         ),
         dict(gain_ffn=gain_row, g_down=down_spec, d_residual=block32),
         need=dict(
-            cotangent=SENT, residual=SENT, few=SENT, rows_ffn=1, hidden=SENT, cat_sums=SENT, shared=1
+            cotangent=SENT, residual=SENT, few=SENT, hidden=SENT, cat_sums=SENT, shared=3
         ),
-        done=dict(gain_ffn=1, d_residual=CHUNK + 3, g_down=SPREAD),
+        done=dict(gain_ffn=3, d_residual=CHUNK + 3, g_down=SPREAD),
         scratch=dict(dgu=pltpu.VMEM((length, 2 * units), B16), g_gu=pltpu.VMEM(*gu_spec)),
-        phases=ffn_bwd_phases, fills=fills_ffn, part_width=depth, gathers=dict(rows_back=0),
+        phases=ffn_back_phases, fills=fills_ffn, scatters={PART: (depth, 4, (0, 1, 2))}, gathers=dict(rows_back=0),
         helpers=hauls,
     )
     gu_sums = hauls[2].result
@@ -1740,16 +1819,16 @@
     first.add(got)
 
     hauls = [
-        Haul(0, dp, [from_input(lambda r: r.gu_sums)], [gu_spec], {BEGIN: 1, 3: 1}, swap=False),
+        Haul(0, dp, [from_input(lambda r: r.gu_sums)], [gu_spec], {BEGIN: 1, 4: 1}, swap=False),
         Haul(
-            0, dp, [from_input(take_down)], [down_spec], {BEGIN: 1, 1: 1, 2: 2, 3: 1, 5: 1}
+            0, dp, [from_input(take_down)], [down_spec], {BEGIN: 1, 1: 1, 2: 2, 3: 1, SENT: 1}
         ),
-        Haul(0, dp, [from_kernel(take_out)], [out_spec], {1: 1, 3: 2, 4: 2, SENT: 1}),
+        Haul(0, dp, [from_kernel(take_out)], [out_spec], {1: 1, 3: 2, 4: 2, CHUNK + 2: 1}),
         Haul(
             0, dp, [from_kernel(take_cat)], [cat_spec],
             {4: 1, 6: 1, SENT: 1, CHUNK: 1, CHUNK + 1: 1},
         ),
-        Straight(0, dp, from_kernel(take_shared), shared_spec, {CHUNK + 3: 1}),
+        Straight(0, dp, from_kernel(take_shared), shared_spec, {EXTRA: 1}),
     ]
     x_grads = Place(
         lambda r: (r.x_grad, r.raw.x_grad1), (rows, depth), 0,
@@ -1759,11 +1838,11 @@
         "back0", 7, functools.partial(work_back_mix, 0),
         dict(core_inputs(first), acts_in=acts_in, x_grad1=second.x_grad, gu_sums=gu_sums, g_down=first.g_down),
         {},
-        need=dict(core_need, x_grad1=None, gu_sums=3, rest=5, gain_ffn=6),
+        need=dict(core_need, x_grad1=None, gu_sums=3),
         scratch=dict(
             core_scratch, **inner, x_grad=pltpu.VMEM(*block16), shared=pltpu.VMEM(*shared_spec)
         ),
-        phases=functools.partial(back_phases, 0), part_width=depth + wide, helpers=hauls + [x_grads],
+        phases=functools.partial(back_phases, 0), scatters=back_scatters, extra_work=work_shared, helpers=hauls + [x_grads],
     )
     first.sums = [h.result for h in hauls]
     order = [0, 1, 3, 2, 4]

time: 523 us -> 505 us (0.966)
  Pallas kernels: 490 us -> 472 us
    pallas_call x8, Pallas kernels: 490 us -> 472 us  [exchange(): pl.pallas_call(functools.partial(exchange_kernel, plan), out_shape=shapes...]
where the time goes in v1:
time: 505 us; the launch traced here: 497 us
  Pallas kernels  472 us (93%)
  local copies, waits for them, and re-layouts  18.5 us (4%)
    pallas_call x8, Pallas kernels, exchange(): pl.pallas_call(functools.partial(exchange_kernel, plan), out_shape=shapes...  472 us

profile of v1, /device:TPU:8, one launch (start us, length us, event | category | flops | bytes accessed | tf_op | source)
XLA Modules:
  0.0 496.6 jit_solution(13239961343270557254)
XLA Ops:
  0.7 0.7 pad.17
  1.4 0.7 pad.18
  2.0 0.7 pad.19
  2.7 0.7 dynamic-slice_bitcast_fusion.1
  3.4 1.9 concatenate.25.refs_2_
  5.4 0.8 slice_bitcast_fusion.8
  6.2 1.9 fusion.8
  8.3 0.7 fusion.7
  9.2 52.4 %first.1 = (bf16[1024,1024]{1,0:T(8,128)(2,1)}, bf16[1024,1024]{1,0:T(8,128)(2,1)}, f32[2,4,16,256]{3,2,1,0:T(8,128)}, bf16[4,1536,256]{2,1,0:T(8,128)(2,1)}, bf16[4,4,128,256]{3,2,1,0:T(8,128)(2,1)}) custom-call(bf16[2,256,1024]{2,1,0:T(8,128)(2,1)} %refs_13_.1, bf16[2,256,1024]{2,1,0:T(8,128)(2,1)} %refs_0_.5, f32[16,256]{1,0:T(8,128)} %concatenate.25.refs_2_, ...), custom_call_target="tpu_custom_call" | custom-call | flops 20000000000 | bytes 50000000 | tf_op jit(solution)/shard_map/first/pallas_call | solution.py:1456
  61.6 53.4 %mixer0.1 = (bf16[1024,1408]{1,0:T(8,128)(2,1)}, f32[1024,128]{1,0:T(8,128)}, bf16[1024,384]{1,0:T(8,128)(2,1)}, bf16[1024,512]{1,0:T(8,128)(2,1)}, bf16[8,128,3...) custom-call(bf16[2,256,1024]{2,1,0:T(8,128)(2,1)} %refs_13_.1, ...), custom_call_target="tpu_custom_call" | custom-call | flops 20000000000 | bytes 50000000 | tf_op jit(solution)/shard_map/mixer0/pallas_call | solution.py:1456
  115.1 49.6 %turn.1 = (bf16[1024,1024]{1,0:T(8,128)(2,1)}, bf16[1024,512]{1,0:T(8,128)(2,1)}, bf16[256,1024]{1,0:T(8,128)(2,1)}, bf16[1024,1024]{1,0:T(8,128)(2,1)}, bf16[4,...) custom-call(f32[256,1024]{1,0:T(8,128)} %get-tuple-element.73.refs_0_.refs_1_, ...), custom_call_target="tpu_custom_call" | custom-call | flops 20000000000 | bytes 50000000 | tf_op jit(solution)/shard_map/turn/pallas_call | solution.py:1456
  164.7 50.3 %mixer1.1 = (bf16[1024,1408]{1,0:T(8,128)(2,1)}, f32[1024,128]{1,0:T(8,128)}, bf16[1024,384]{1,0:T(8,128)(2,1)}, bf16[1024,512]{1,0:T(8,128)(2,1)}, bf16[8,128,3...) custom-call(bf16[256,1024]{1,0:T(8,128)(2,1)} %get-tuple-element.76., ...), custom_call_target="tpu_custom_call" | custom-call | flops 20000000000 | bytes 50000000 | tf_op jit(solution)/shard_map/mixer1/pallas_call | solution.py:1456
  214.9 51.0 %ffn1.1 = (f32[8,1024]{1,0:T(8,128)}, bf16[2,4,128,1024]{3,2,1,0:T(8,128)(2,1)}, bf16[2,4,256,256]{3,2,1,0:T(8,128)(2,1)}, f32[256,1024]{1,0:T(8,128)}, bf16[102...) custom-call(bf16[2,256,1024]{2,1,0:T(8,128)(2,1)} %refs_0_.5, f32[256,1024]{1,0:T(8,128)} %get-tuple-element.80.refs_1_, ...), custom_call_target="tpu_custom_call" | custom-call | flops 20000000000 | bytes 50000000 | tf_op jit(solution)/shard_map/ffn1/pallas_call | solution.py:1456
  265.9 76.4 %back1.1 = (bf16[256,1024]{1,0:T(8,128)(2,1)}, f32[2,4,32,640]{3,2,1,0:T(8,128)}, bf16[1024,1024]{1,0:T(8,128)(2,1)}, bf16[2,128,1024]{2,1,0:T(8,128)(2,1)}, bf1...) custom-call(f32[2,4,16,256]{3,2,1,0:T(8,128)} %get-tuple-element.69.refs_1_.refs_2_.refs_0_, ...), custom_call_target="tpu_custom_call" | custom-call | flops 20000000000 | bytes 50000000 | tf_op jit(solution)/shard_map/back1/pallas_call | solution.py:1456
  342.3 43.8 %ffn0.1 = (f32[8,1024]{1,0:T(8,128)}, bf16[2,4,256,256]{3,2,1,0:T(8,128)(2,1)}, f32[256,1024]{1,0:T(8,128)}, bf16[1024,1024]{1,0:T(8,128)(2,1)}, bf16[2,128,896]...) custom-call(bf16[256,1024]{1,0:T(8,128)(2,1)} %get-tuple-element.97.refs_0_.refs_14_, ...), custom_call_target="tpu_custom_call" | custom-call | flops 20000000000 | bytes 50000000 | tf_op jit(solution)/shard_map/ffn0/pallas_call | solution.py:1456
  386.1 95.4 %back0.1 = (bf16[2,128,1024]{2,1,0:T(8,128)(2,1)}, bf16[2,256,256]{2,1,0:T(8,128)(2,1)}, bf16[2,256,256]{2,1,0:T(8,128)(2,1)}, bf16[2,128,896]{2,1,0:T(8,128)(2,...) custom-call(f32[2,4,16,256]{3,2,1,0:T(8,128)} %get-tuple-element.69.refs_1_.refs_2_.refs_0_, ...), custom_call_target="tpu_custom_call" | custom-call | flops 20000000000 | bytes 50000000 | tf_op jit(solution)/shard_map/back0/pallas_call | solution.py:1456
  481.6 1.1 broadcast_select_fusion.1
  482.7 1.0 broadcast_select_fusion.2
  483.7 1.1 broadcast_select_fusion
  485.0 1.9 reshape.54
  486.9 0.6 copy.45
  487.5 0.7 copy.52
  488.2 0.7 slice_bitcast_fusion.4
  488.9 0.6 copy.42
  489.6 0.7 slice_bitcast_fusion.3
  490.2 0.8 slice_bitcast_fusion
  491.0 0.8 bitcast_convert_fusion.1
  491.8 0.1 bitcast_convert_fusion
  491.9 0.7 slice_bitcast_fusion.5
  492.7 1.5 copy.44
  494.2 1.0 copy.79
  495.2 1.0 copy.80
  (59 shorter events, 0.8 us)
Async XLA Ops:
  0.6 4.7 copy-start
  5.3 2.9 copy-start.11
  6.2 2.1 copy-start.14
  6.2 2.1 copy-start.2
  8.2 1.0 copy-start.8
  8.3 0.9 copy-start.16
  9.2 52.4 %copy-start.15 = (bf16[1536,256]{1,0:T(8,128)(2,1)}, bf16[1536,256]{1,0:T(8,128)(2,1)S(1)}, u32[]{:S(2)}) copy-start(bf16[1536,256]{1,0:T(8,128)(2,1)S(1)} %bitcast_dynamic-update-slice_fusion.refs_5_) | copy-start | bytes 2359300
  386.1 95.5 %copy-start.10 = (bf16[2,256,256]{2,1,0:T(8,128)(2,1)S(1)}, bf16[2,256,256]{2,1,0:T(8,128)(2,1)}, u32[]{:S(2)}) copy-start(bf16[2,256,256]{2,1,0:T(8,128)(2,1)} %get-tuple-element.125) | copy-start | bytes 786436
  386.1 96.6 %copy-start.9 = (bf16[2,256,256]{2,1,0:T(8,128)(2,1)S(1)}, bf16[2,256,256]{2,1,0:T(8,128)(2,1)}, u32[]{:S(2)}) copy-start(bf16[2,256,256]{2,1,0:T(8,128)(2,1)} %get-tuple-element.121) | copy-start | bytes 786436
  386.1 97.6 %copy-start.7 = (bf16[2,128,896]{2,1,0:T(8,128)(2,1)S(1)}, bf16[2,128,896]{2,1,0:T(8,128)(2,1)}, u32[]{:S(2)}) copy-start(bf16[2,128,896]{2,1,0:T(8,128)(2,1)} %get-tuple-element.119) | copy-start | bytes 1376260
  481.6 3.2 copy-start.12
  481.6 3.2 copy-start.13
  481.6 3.3 copy-start.5
  481.6 3.3 copy-start.6
  492.6 1.6 copy-start.3
  492.7 2.5 copy-start.4
  492.7 3.4 copy-start.1

commit v2 on v1

--- a/solution.py
+++ b/solution.py
@@ -1542,7 +1542,7 @@
     total = scatters[SHARED].receive(0)
     _, ways, block, _ = r.shared.shape
     for j in range(2 * ways):
-        r.shared[j // ways, j % ways] = total[j * block : (j + 1) * block, :]
+        r.shared[j // ways, j % ways] = total[j * block : (j + 1) * block, :].astype(r.shared.dtype)
 
 
 def widen(block, axis, size):
@@ -1593,9 +1593,11 @@
         axis=0,
     )
     few_shard = jnp.concatenate(
-        [mix_gain.astype(F32), ffn_gain.astype(F32)]
-        + [widen(row, 1, piece) for row in (a_log, dt_bias, d_skip)]
-        + [jnp.zeros((3, piece), F32), widen(steps, 0, 8)],
+        [
+            mix_gain.astype(F32), ffn_gain.astype(F32),
+            widen(widen(jnp.concatenate([a_log, dt_bias, d_skip]), 1, piece), 0, 6),
+            widen(steps, 0, 8),
+        ],
         axis=0,
     )
 
@@ -1616,7 +1618,7 @@
     ffn_keeps = dict(gu=((length, 2 * units), B16), hidden=((length, units), B16))
     gu_spec, down_spec = ((2, dp, half, 2 * units), B16), ((2, dp, units // 2, piece), B16)
     cat_spec, out_spec = ((2, dp, half, cols.b), B16), ((2, dp, low_units // 2, piece), B16)
-    shared_spec = ((2, dp, half // members, wide), F32)
+    shared_spec = ((2, dp, half // members, wide), B16 if half // members % 16 == 0 else F32)
     gain_row = ((8, depth), F32)
     fills_ffn = [
         lambda r: grad_columns(r.rows_ffn, r.dgu, r.g_gu),
@@ -1630,7 +1632,7 @@
         {BEGIN: 1, SENT: 2, CHUNK: 1, CHUNK + 1: 1, CHUNK + 2: 2, CHUNK + 3: 2, SPREAD: 2, GIVEN: 4},
         members, at_row.shared,
     )
-    few = Few(dp, few_shard, {BEGIN: 3})
+    few = Few(dp, few_shard, {BEGIN: 2, SENT: 1})
     got = run(
         "first", 0, work_first, dict(acts_in=acts_in, out_grad=out_grad), {},
         gathers=dict(rows_mix=0, rows_out=0), helpers=[few, load],
@@ -1643,8 +1645,8 @@
         load = Cargo(
             layer, dp, ffn_shard,
             {
-                BEGIN: 1, 0: 1, 1: 1, 2: 1, 3: 2, 4: 1, 5: 1, 6: 1, 7: 2, SENT: 1, CHUNK: 1, CHUNK + 1: 1,
-                CHUNK + 2: 1, CHUNK + 3: 1, SPREAD: 2,
+                BEGIN: 1, 0: 1, 1: 1, 2: 1, 3: 2, 4: 1, 5: 1, 6: 2, 7: 2, SENT: 1, CHUNK: 1, CHUNK + 1: 1,
+                CHUNK + 2: 1, SPREAD: 2,
             },
         )
         k.add(

time: 505 us -> 491 us (0.972)
  Pallas kernels: 472 us -> 460 us
    pallas_call x8, Pallas kernels: 472 us -> 460 us  [exchange(): pl.pallas_call(functools.partial(exchange_kernel, plan), out_shape=shapes...]
where the time goes in v2:
time: 491 us; the launch traced here: 483 us
  Pallas kernels  460 us (94%)
  local copies, waits for them, and re-layouts  14.6 us (3%)
  other arithmetic  7.05 us (1%)
    pallas_call x8, Pallas kernels, exchange(): pl.pallas_call(functools.partial(exchange_kernel, plan), out_shape=shapes...  460 us

profile of v2, /device:TPU:8, one launch (start us, length us, event | category | flops | bytes accessed | tf_op | source)
XLA Modules:
  0.0 482.8 jit_solution(4507543773348458869)
XLA Ops:
  0.7 0.7 convert_element_type.24
  1.4 0.7 convert_element_type.25
  2.1 0.7 dynamic-slice_bitcast_fusion.1
  2.8 0.7 select_maximum_fusion.1
  3.5 0.6 fusion.7.refs_2_
  4.1 0.8 slice_bitcast_fusion.8
  5.0 1.9 fusion.10
  7.1 0.7 fusion.9
  8.0 49.4 %first.1 = (bf16[1024,1024]{1,0:T(8,128)(2,1)}, bf16[1024,1024]{1,0:T(8,128)(2,1)}, f32[2,4,16,256]{3,2,1,0:T(8,128)}, bf16[4,1536,256]{2,1,0:T(8,128)(2,1)}, bf16[4,4,128,256]{3,2,1,0:T(8,128)(2,1)}) custom-call(bf16[2,256,1024]{2,1,0:T(8,128)(2,1)} %refs_13_.1, bf16[2,256,1024]{2,1,0:T(8,128)(2,1)} %refs_0_.5, f32[16,256]{1,0:T(8,128)} %fusion.7.refs_2_, ...), custom_call_target="tpu_custom_call" | custom-call | flops 20000000000 | bytes 50000000 | tf_op jit(solution)/shard_map/first/pallas_call | solution.py:1456
  57.4 52.3 %mixer0.1 = (bf16[1024,1408]{1,0:T(8,128)(2,1)}, f32[1024,128]{1,0:T(8,128)}, bf16[1024,384]{1,0:T(8,128)(2,1)}, bf16[1024,512]{1,0:T(8,128)(2,1)}, bf16[8,128,3...) custom-call(bf16[2,256,1024]{2,1,0:T(8,128)(2,1)} %refs_13_.1, ...), custom_call_target="tpu_custom_call" | custom-call | flops 20000000000 | bytes 50000000 | tf_op jit(solution)/shard_map/mixer0/pallas_call | solution.py:1456
  109.7 49.4 %turn.1 = (bf16[1024,1024]{1,0:T(8,128)(2,1)}, bf16[1024,512]{1,0:T(8,128)(2,1)}, bf16[256,1024]{1,0:T(8,128)(2,1)}, bf16[1024,1024]{1,0:T(8,128)(2,1)}, bf16[4,...) custom-call(f32[256,1024]{1,0:T(8,128)} %get-tuple-element.73.refs_0_.refs_1_, ...), custom_call_target="tpu_custom_call" | custom-call | flops 20000000000 | bytes 50000000 | tf_op jit(solution)/shard_map/turn/pallas_call | solution.py:1456
  159.1 50.8 %mixer1.1 = (bf16[1024,1408]{1,0:T(8,128)(2,1)}, f32[1024,128]{1,0:T(8,128)}, bf16[1024,384]{1,0:T(8,128)(2,1)}, bf16[1024,512]{1,0:T(8,128)(2,1)}, bf16[8,128,3...) custom-call(bf16[256,1024]{1,0:T(8,128)(2,1)} %get-tuple-element.76., ...), custom_call_target="tpu_custom_call" | custom-call | flops 20000000000 | bytes 50000000 | tf_op jit(solution)/shard_map/mixer1/pallas_call | solution.py:1456
  209.9 48.5 %ffn1.1 = (f32[8,1024]{1,0:T(8,128)}, bf16[2,4,128,1024]{3,2,1,0:T(8,128)(2,1)}, bf16[2,4,256,256]{3,2,1,0:T(8,128)(2,1)}, f32[256,1024]{1,0:T(8,128)}, bf16[102...) custom-call(bf16[2,256,1024]{2,1,0:T(8,128)(2,1)} %refs_0_.5, f32[256,1024]{1,0:T(8,128)} %get-tuple-element.80.refs_1_, ...), custom_call_target="tpu_custom_call" | custom-call | flops 20000000000 | bytes 50000000 | tf_op jit(solution)/shard_map/ffn1/pallas_call | solution.py:1456
  258.4 76.5 %back1.1 = (bf16[256,1024]{1,0:T(8,128)(2,1)}, bf16[2,4,32,640]{3,2,1,0:T(8,128)(2,1)}, bf16[1024,1024]{1,0:T(8,128)(2,1)}, bf16[2,128,1024]{2,1,0:T(8,128)(2,1)...) custom-call(f32[2,4,16,256]{3,2,1,0:T(8,128)} %get-tuple-element.69.refs_1_.refs_2_.refs_, ...), custom_call_target="tpu_custom_call" | custom-call | flops 20000000000 | bytes 50000000 | tf_op jit(solution)/shard_map/back1/pallas_call | solution.py:1456
  334.9 42.9 %ffn0.1 = (f32[8,1024]{1,0:T(8,128)}, bf16[2,4,256,256]{3,2,1,0:T(8,128)(2,1)}, f32[256,1024]{1,0:T(8,128)}, bf16[1024,1024]{1,0:T(8,128)(2,1)}, bf16[2,128,896]...) custom-call(bf16[256,1024]{1,0:T(8,128)(2,1)} %get-tuple-element.97.refs_0_.refs_14_, ...), custom_call_target="tpu_custom_call" | custom-call | flops 20000000000 | bytes 50000000 | tf_op jit(solution)/shard_map/ffn0/pallas_call | solution.py:1456
  377.7 90.0 %back0.1 = (bf16[2,128,1024]{2,1,0:T(8,128)(2,1)}, bf16[2,256,256]{2,1,0:T(8,128)(2,1)}, bf16[2,256,256]{2,1,0:T(8,128)(2,1)}, bf16[2,128,896]{2,1,0:T(8,128)(2,...) custom-call(f32[2,4,16,256]{3,2,1,0:T(8,128)} %get-tuple-element.69.refs_1_.refs_2_.refs_0_, ...), custom_call_target="tpu_custom_call" | custom-call | flops 20000000000 | bytes 50000000 | tf_op jit(solution)/shard_map/back0/pallas_call | solution.py:1456
  467.8 1.1 broadcast_select_fusion.1
  468.9 1.0 broadcast_select_fusion.2
  469.9 1.1 broadcast_select_fusion
  471.2 1.9 reshape.60
  473.1 0.6 copy.45
  473.7 0.7 copy.52
  474.4 0.7 slice_bitcast_fusion.4
  475.1 0.6 copy.42
  475.8 0.7 slice_bitcast_fusion.3
  476.5 0.8 slice_bitcast_fusion
  477.2 0.8 bitcast_convert_fusion.1
  478.1 0.1 bitcast_convert_fusion
  478.2 0.7 slice_bitcast_fusion.5
  479.0 1.5 copy.44
  480.5 1.0 copy.79
  481.4 1.0 copy.80
  (59 shorter events, 0.8 us)
Async XLA Ops:
  0.6 3.5 copy-start
  4.1 2.9 copy-start.11
  5.0 2.1 copy-start.14
  5.0 2.1 copy-start.2
  7.0 1.0 copy-start.8
  7.1 0.9 copy-start.16
  8.0 49.4 %copy-start.15 = (bf16[1536,256]{1,0:T(8,128)(2,1)}, bf16[1536,256]{1,0:T(8,128)(2,1)S(1)}, u32[]{:S(2)}) copy-start(bf16[1536,256]{1,0:T(8,128)(2,1)S(1)} %bitcast_dynamic-update-slice_fusion.refs_5_) | copy-start | bytes 2359300
  377.7 90.1 %copy-start.10 = (bf16[2,256,256]{2,1,0:T(8,128)(2,1)S(1)}, bf16[2,256,256]{2,1,0:T(8,128)(2,1)}, u32[]{:S(2)}) copy-start(bf16[2,256,256]{2,1,0:T(8,128)(2,1)} %get-tuple-element.125) | copy-start | bytes 786436
  377.7 91.2 %copy-start.9 = (bf16[2,256,256]{2,1,0:T(8,128)(2,1)S(1)}, bf16[2,256,256]{2,1,0:T(8,128)(2,1)}, u32[]{:S(2)}) copy-start(bf16[2,256,256]{2,1,0:T(8,128)(2,1)} %get-tuple-element.121) | copy-start | bytes 786436
  377.7 92.2 %copy-start.7 = (bf16[2,128,896]{2,1,0:T(8,128)(2,1)S(1)}, bf16[2,128,896]{2,1,0:T(8,128)(2,1)}, u32[]{:S(2)}) copy-start(bf16[2,128,896]{2,1,0:T(8,128)(2,1)} %get-tuple-element.119) | copy-start | bytes 1376260
  467.8 3.2 copy-start.12
  467.8 3.2 copy-start.13
  467.8 3.3 copy-start.5
  467.8 3.3 copy-start.6
  478.8 1.6 copy-start.3
  478.9 2.5 copy-start.4
  479.0 3.4 copy-start.1

commit v3 on v2

--- a/solution.py
+++ b/solution.py
@@ -141,12 +141,12 @@
     return total
 
 
-def multiply_out(lows_ref, weights_ref, first, part_ref, rows, at=0):
+def multiply_out(lows_ref, weights_ref, first, part_ref, rows):
     ways, _, piece = weights_ref.shape
     last = first + lows_ref.shape[1]
     block = lows_ref[rows, :]
     for k in range(ways):
-        part_ref[rows, at + k * piece : at + (k + 1) * piece] = nn(
+        part_ref[rows, k * piece : (k + 1) * piece] = nn(
             block, weights_ref[k, first:last, :]
         ).astype(B16)
 
@@ -572,7 +572,7 @@
     return [into_all, attend_all, scan_all, shared_all] + by_blocks(order, length // members, back)
 
 
-def ffn_forward(r, rows, at=0):
+def ffn_forward(r, rows, part_ref):
     rows_ref, weights_ref, gu_ref, hidden_ref = r.rows_ffn, r.gates, r.gu, r.hidden
     units = hidden_ref.shape[1]
     piece = weights_ref.shape[2]
@@ -584,7 +584,7 @@
         gu_ref[rows, to] = g.astype(B16)
         gu_ref[rows, units + c * piece : units + (c + 1) * piece] = v.astype(B16)
         hidden_ref[rows, to] = (g * sigmoid(g) * v).astype(B16)
-    multiply_out(hidden_ref, weights_ref, 2 * units, r.part, rows, at)
+    multiply_out(hidden_ref, weights_ref, 2 * units, part_ref, rows)
 
 
 def ffn_backward(r, rows):
@@ -646,7 +646,7 @@
 DMA = pltpu.SemaphoreType.DMA
 MESH = pl.DeviceIdType.MESH
 PIPE, DP, TENSOR = "pipe", "dp", "tensor"
-PART, SHARED = "part", "extra"
+PART, SHARED, LAST = "part", "extra", "ffn_part"
 
 BEGIN, SENT, EXTRA, CHUNK, SPREAD, GIVEN, END = -1, 20, 25, 30, 40, 50, 60
 
@@ -928,8 +928,7 @@
                     send_far(count, pairs - count).wait_send()
             own_share().wait()
 
-        at = len(steps) - (chunks - 1)
-        return steps[:at] + [share_out] + steps[at:] + [pass_on, finish_all]
+        return steps + [share_out, pass_on, finish_all]
 
 
 class Haul(Helper):
@@ -1164,6 +1163,45 @@
         return [early] + [functools.partial(hand, self.late, c) for c in range(self.PIECES)] + [finish]
 
 
+class Settle(Helper):
+    def __init__(self, layer, source, shape, when):
+        super().__init__(when)
+        self.layer, self.source = layer, source
+        self.outs = [((2,) + shape, B16, pl.ANY)]
+        self.scratch = [DMA((1,)), DMA((1,)), DMA((1,))]
+
+    def bind(self, r, inputs, outs, scratch):
+        (out,) = outs
+        send, receive, local = scratch
+        section = lax.axis_index(PIPE)
+        rows = self.source(r)
+        owner = section == self.layer
+
+        def over():
+            return remote(
+                rows, out.at[1 - self.layer], send.at[0], receive.at[0], {PIPE: 1 - section}
+            )
+
+        def own():
+            return pltpu.make_async_copy(rows, out.at[self.layer], local.at[0])
+
+        def start():
+            pl.when(section != self.layer)(lambda: over().start())
+            pl.when(owner)(lambda: own().start())
+
+        def finish():
+            @pl.when(section != self.layer)
+            def _():
+                over().wait_send()
+
+            @pl.when(owner)
+            def _():
+                over().wait_recv()
+                own().wait()
+
+        return [start, finish]
+
+
 class Members:
     def __init__(self, count):
         self.pairs = count // 2
@@ -1279,7 +1317,8 @@
     pairs, pieces = at.pairs, plan.pieces
     scatters = {}
     for name, (_, count, _) in plan.scatters.items():
-        setattr(r, name, take(1)[0])
+        if name not in plan.inputs:
+            setattr(r, name, take(1)[0])
         scatters[name] = Scatter(getattr(r, name), at, plan.rows, count, take(7))
     if plan.gathers:
         mine_refs = take(len(plan.gathers))
@@ -1434,8 +1473,9 @@
     staging += [pltpu.VMEM(*spec) for spec in outs.values()]
     staging += list(scratch.values())
     staging += [DMA((max(len(inputs), 1),)), DMA((max(len(outs), 1),))]
-    for width, chunks, _ in scatters.values():
-        staging.append(pltpu.VMEM((members * rows, width), B16))
+    for part, (width, chunks, _) in scatters.items():
+        if part not in inputs:
+            staging.append(pltpu.VMEM((members * rows, width), B16))
         staging += Scatter.scratch(members, rows, width, chunks)
     count = len(gathers)
     if count:
@@ -1520,12 +1560,9 @@
 
 
 def work_back_ffn(layer, r, c, at, total):
-    depth = r.residual.shape[1]
     residual = r.residual[at, :]
-    if layer == 1:
-        r.last[at, :] = (residual + total[:, depth:]).astype(B16)
     grad = layer_cotangent(r, layer, at).astype(F32) + rms_back(
-        residual, gain_of(r, layer, 1), total[:, :depth]
+        residual, gain_of(r, layer, 1), total
     )
     r.d_residual[at, :] = grad
     return (grad.astype(B16),)
@@ -1543,6 +1580,11 @@
     _, ways, block, _ = r.shared.shape
     for j in range(2 * ways):
         r.shared[j // ways, j % ways] = total[j * block : (j + 1) * block, :].astype(r.shared.dtype)
+
+
+def work_last(r, scatters):
+    r.last[...] = (r.residual[...] + scatters[LAST].receive(0)).astype(B16)
+    work_shared(r, scatters)
 
 
 def widen(block, axis, size):
@@ -1676,7 +1718,7 @@
                 dict(residual=k.residual, few=few, rows_ffn=k.rows_ffn, gates=k.gates),
                 dict(ffn_keeps, x=block16),
                 need=dict(residual=SENT, few=SENT), done=dict(gu=3, hidden=3, x=CHUNK + 3),
-                phases=lambda r, order: by_blocks(order, rows, lambda at, m: ffn_forward(r, at)),
+                phases=lambda r, order: by_blocks(order, rows, lambda at, m: ffn_forward(r, at, r.part)),
                 scatters={PART: (depth, 4, (0, 1, 2))}, gathers=dict(rows_mix=0), helpers=[load],
             )
             k.gu, k.hidden = got.gu, got.hidden
@@ -1687,7 +1729,7 @@
         r.gain_ffn[...] = jnp.zeros_like(r.gain_ffn)
 
     def ffn_both(r, at, m):
-        ffn_forward(r, at, depth)
+        ffn_forward(r, at, r.ffn_part)
         ffn_backward(r, at)
 
     def ffn_both_phases(r, order):
@@ -1698,27 +1740,25 @@
         clear_gain(r)
         return by_blocks(order, rows, lambda at, m: ffn_backward(r, at))
 
-    acts = Place(
-        lambda r: (r.raw.x, r.last), (rows, depth), 1,
-        {BEGIN: 1, CHUNK: 1, CHUNK + 1: 1, CHUNK + 2: 1, CHUNK + 3: 1},
-    )
     second.add(
         run(
             "ffn1", 4, functools.partial(work_back_ffn, 1),
             dict(
                 out_grad=out_grad, residual=second.residual, few=few, rows_ffn=second.rows_ffn,
-                rows_out=second.rows_out, gates=second.gates, x=second.x,
+                rows_out=second.rows_out, gates=second.gates,
             ),
-            dict(gain_ffn=gain_row, g_gu=gu_spec, g_down=down_spec, d_residual=block32),
-            need=dict(out_grad=SENT, residual=SENT, few=SENT, x=None),
-            done=dict(gain_ffn=3, g_gu=SENT, d_residual=CHUNK + 3, g_down=SPREAD),
+            dict(
+                gain_ffn=gain_row, g_gu=gu_spec, g_down=down_spec, d_residual=block32,
+                ffn_part=((length, depth), B16),
+            ),
+            need=dict(out_grad=SENT, residual=SENT, few=SENT),
+            done=dict(ffn_part=3, gain_ffn=3, g_gu=SENT, d_residual=CHUNK + 3, g_down=SPREAD),
             scratch=dict(
-                last=pltpu.VMEM(*block16),
                 **{n: pltpu.VMEM(*spec) for n, spec in ffn_keeps.items()},
                 dgu=pltpu.VMEM((length, 2 * units), B16),
             ),
             phases=ffn_both_phases,
-            scatters={PART: (2 * depth, 4, (0, 1, 2))}, fills=fills_ffn, gathers=dict(rows_back=0), helpers=[acts],
+            scatters={PART: (depth, 4, (0, 1, 2))}, fills=fills_ffn, gathers=dict(rows_back=0),
         )
     )
 
@@ -1759,6 +1799,7 @@
     take_gu, take_down = (lambda r: r.g_gu), (lambda r: r.g_down)
     take_cat, take_out, take_shared = (lambda r: r.g_cat), (lambda r: r.g_out), (lambda r: r.shared)
 
+    first_acts = Settle(0, lambda r: r.raw.x, (rows, depth), {SENT: 1})
     def back_phases(layer, r, order):
         into, attend, scan, shared, *back = core_phases(layer, r, order)
         return [into, lambda: fill_out(r), attend, scan, lambda: fill_cat(r), shared] + back
@@ -1777,12 +1818,15 @@
     inner = dict(g_cat=pltpu.VMEM(*cat_spec), g_out=pltpu.VMEM(*out_spec))
     got = run(
         "back1", 5, functools.partial(work_back_mix, 1),
-        dict(core_inputs(second), x=second.x, g_gu=second.g_gu, g_down=second.g_down),
-        dict(x_grad=block16, shared=shared_spec),
-        need=core_need,
-        done=dict(x_grad=CHUNK + 3, shared=EXTRA),
+        dict(
+            core_inputs(second), x=second.x, g_gu=second.g_gu, g_down=second.g_down, ffn_part=second.ffn_part,
+            residual=second.residual,
+        ),
+        dict(x_grad=block16, shared=shared_spec, last=block16),
+        need=dict(core_need, residual=SENT),
+        done=dict(x_grad=CHUNK + 3, shared=EXTRA, last=EXTRA),
         scratch=dict(core_scratch, **inner), phases=functools.partial(back_phases, 1),
-        scatters=back_scatters, extra_work=work_shared, gathers=dict(rows_out=0), helpers=hauls,
+        scatters=dict(back_scatters, ffn_part=(depth, 1, (0, 1, 0))), extra_work=work_last, gathers=dict(rows_out=0), helpers=hauls + [first_acts],
     )
     second.add(got)
     cat_sums = hauls[2].result
@@ -1836,15 +1880,17 @@
         lambda r: (r.x_grad, r.raw.x_grad1), (rows, depth), 0,
         {4: 1, CHUNK: 1, CHUNK + 1: 1, CHUNK + 2: 1, CHUNK + 3: 1},
     )
+    second_acts = Settle(1, lambda r: r.raw.last, (rows, depth), {5: 1})
     run(
         "back0", 7, functools.partial(work_back_mix, 0),
-        dict(core_inputs(first), acts_in=acts_in, x_grad1=second.x_grad, gu_sums=gu_sums, g_down=first.g_down),
+        dict(core_inputs(first), acts_in=acts_in, x_grad1=second.x_grad, gu_sums=gu_sums, g_down=first.g_down,
+            last=second.last),
         {},
-        need=dict(core_need, x_grad1=None, gu_sums=3),
+        need=dict(core_need, x_grad1=None, gu_sums=3, last=None),
         scratch=dict(
             core_scratch, **inner, x_grad=pltpu.VMEM(*block16), shared=pltpu.VMEM(*shared_spec)
         ),
-        phases=functools.partial(back_phases, 0), scatters=back_scatters, extra_work=work_shared, helpers=hauls + [x_grads],
+        phases=functools.partial(back_phases, 0), scatters=back_scatters, extra_work=work_shared, helpers=hauls + [x_grads, second_acts],
     )
     first.sums = [h.result for h in hauls]
     order = [0, 1, 3, 2, 4]
@@ -1859,7 +1905,7 @@
     g_gains = g_shared[:, table + GAINS_AT : table + GAINS_AT + 2].T
     g_heads = g_shared[:3, table + HEADS_AT : table + HEADS_AT + heads]
     return (
-        acts.result[None],
+        jnp.where(section == 0, first_acts.result, second_acts.result)[None],
         x_grads.result[None],
         g_gains[None],
         g_mixer[None],

time: 491 us -> 480 us (0.978)
  Pallas kernels: 460 us -> 449 us
    pallas_call x8, Pallas kernels: 460 us -> 449 us  [exchange(): pl.pallas_call(functools.partial(exchange_kernel, plan), out_shape=shapes...]
where the time goes in v3:
time: 480 us; the launch traced here: 473 us
  Pallas kernels  449 us (94%)
  local copies, waits for them, and re-layouts  13.6 us (3%)
  other arithmetic  8.27 us (2%)
    pallas_call x8, Pallas kernels, exchange(): pl.pallas_call(functools.partial(exchange_kernel, plan), out_shape=shapes...  449 us

profile of v3, /device:TPU:8, one launch (start us, length us, event | category | flops | bytes accessed | tf_op | source)
XLA Modules:
  0.0 472.6 jit_solution(10844612182818820777)
XLA Ops:
  0.7 0.7 convert_element_type.24
  1.4 0.7 convert_element_type.25
  2.1 0.7 dynamic-slice_bitcast_fusion.1
  2.8 0.7 select_maximum_fusion.1
  3.5 0.6 fusion.7.refs_2_
  4.1 0.8 slice_bitcast_fusion.8
  5.0 1.9 fusion.10
  7.1 0.7 fusion.9
  8.0 49.4 %first.1 = (bf16[1024,1024]{1,0:T(8,128)(2,1)}, bf16[1024,1024]{1,0:T(8,128)(2,1)}, f32[2,4,16,256]{3,2,1,0:T(8,128)}, bf16[4,1536,256]{2,1,0:T(8,128)(2,1)}, bf16[4,4,128,256]{3,2,1,0:T(8,128)(2,1)}) custom-call(bf16[2,256,1024]{2,1,0:T(8,128)(2,1)} %refs_13_.1, bf16[2,256,1024]{2,1,0:T(8,128)(2,1)} %refs_0_.5, f32[16,256]{1,0:T(8,128)} %fusion.7.refs_2_, ...), custom_call_target="tpu_custom_call" | custom-call | flops 20000000000 | bytes 50000000 | tf_op jit(solution)/shard_map/first/pallas_call | solution.py:1496
  57.4 52.3 %mixer0.1 = (bf16[1024,1408]{1,0:T(8,128)(2,1)}, f32[1024,128]{1,0:T(8,128)}, bf16[1024,384]{1,0:T(8,128)(2,1)}, bf16[1024,512]{1,0:T(8,128)(2,1)}, bf16[8,128,3...) custom-call(bf16[2,256,1024]{2,1,0:T(8,128)(2,1)} %refs_13_.1, ...), custom_call_target="tpu_custom_call" | custom-call | flops 20000000000 | bytes 50000000 | tf_op jit(solution)/shard_map/mixer0/pallas_call | solution.py:1496
  109.7 49.5 %turn.1 = (bf16[1024,1024]{1,0:T(8,128)(2,1)}, bf16[1024,512]{1,0:T(8,128)(2,1)}, bf16[256,1024]{1,0:T(8,128)(2,1)}, bf16[1024,1024]{1,0:T(8,128)(2,1)}, bf16[4,...) custom-call(f32[256,1024]{1,0:T(8,128)} %get-tuple-element.76.refs_0_.refs_1_, ...), custom_call_target="tpu_custom_call" | custom-call | flops 20000000000 | bytes 50000000 | tf_op jit(solution)/shard_map/turn/pallas_call | solution.py:1496
  159.2 50.0 %mixer1.1 = (bf16[1024,1408]{1,0:T(8,128)(2,1)}, f32[1024,128]{1,0:T(8,128)}, bf16[1024,384]{1,0:T(8,128)(2,1)}, bf16[1024,512]{1,0:T(8,128)(2,1)}, bf16[8,128,3...) custom-call(bf16[256,1024]{1,0:T(8,128)(2,1)} %get-tuple-element.81., ...), custom_call_target="tpu_custom_call" | custom-call | flops 20000000000 | bytes 50000000 | tf_op jit(solution)/shard_map/mixer1/pallas_call | solution.py:1496
  209.2 33.7 %ffn1.1 = (f32[8,1024]{1,0:T(8,128)}, bf16[2,4,128,1024]{3,2,1,0:T(8,128)(2,1)}, bf16[2,4,256,256]{3,2,1,0:T(8,128)(2,1)}, f32[256,1024]{1,0:T(8,128)}, bf16[102...) custom-call(bf16[2,256,1024]{2,1,0:T(8,128)(2,1)} %refs_0_.5, f32[256,1024]{1,0:T(8,128)} %get-tuple-element.83.refs_1_.refs_17_, ...), custom_call_target="tpu_custom_call" | custom-call | flops 20000000000 | bytes 50000000 | tf_op jit(solution)/shard_map/ffn1/pallas_call | solution.py:1496
  242.9 80.9 %back1.1 = (bf16[256,1024]{1,0:T(8,128)(2,1)}, bf16[2,4,32,640]{3,2,1,0:T(8,128)(2,1)}, bf16[256,1024]{1,0:T(8,128)(2,1)}, bf16[1024,1024]{1,0:T(8,128)(2,1)}, b...) custom-call(f32[2,4,16,256]{3,2,1,0:T(8,128)} %get-tuple-element.72., ...), custom_call_target="tpu_custom_call" | custom-call | flops 20000000000 | bytes 50000000 | tf_op jit(solution)/shard_map/back1/pallas_call | solution.py:1496
  323.8 43.0 %ffn0.1 = (f32[8,1024]{1,0:T(8,128)}, bf16[2,4,256,256]{3,2,1,0:T(8,128)(2,1)}, f32[256,1024]{1,0:T(8,128)}, bf16[1024,1024]{1,0:T(8,128)(2,1)}, bf16[2,128,896]...) custom-call(bf16[256,1024]{1,0:T(8,128)(2,1)} %get-tuple-element.101.refs_0_.refs_14_, ...), custom_call_target="tpu_custom_call" | custom-call | flops 20000000000 | bytes 50000000 | tf_op jit(solution)/shard_map/ffn0/pallas_call | solution.py:1496
  366.8 90.5 %back0.1 = (bf16[2,128,1024]{2,1,0:T(8,128)(2,1)}, bf16[2,256,256]{2,1,0:T(8,128)(2,1)}, bf16[2,256,256]{2,1,0:T(8,128)(2,1)}, bf16[2,128,896]{2,1,0:T(8,128)(2,...) custom-call(f32[2,4,16,256]{3,2,1,0:T(8,128)} %get-tuple-element.72.refs_1_.refs_2_.re, ...), custom_call_target="tpu_custom_call" | custom-call | flops 20000000000 | bytes 50000000 | tf_op jit(solution)/shard_map/back0/pallas_call | solution.py:1496
  457.3 1.1 broadcast_select_fusion.1
  458.5 1.0 broadcast_select_fusion.2
  459.5 1.2 broadcast_select_fusion
  460.7 1.1 select_bitcast_fusion
  461.9 1.9 reshape.60
  463.8 0.6 copy.45
  464.4 0.7 copy.52
  465.2 0.7 slice_bitcast_fusion.4
  465.8 0.6 copy.42
  466.5 0.7 slice_bitcast_fusion.3
  467.2 0.8 slice_bitcast_fusion
  468.0 0.8 bitcast_convert_fusion.1
  468.8 0.1 bitcast_convert_fusion
  468.9 0.7 slice_bitcast_fusion.5
  469.7 1.5 copy.44
  471.2 1.0 copy.78
  (61 shorter events, 0.8 us)
Async XLA Ops:
  0.6 3.5 copy-start
  4.1 2.9 copy-start.12
  5.0 2.1 copy-start.15
  5.0 2.1 copy-start.2
  7.0 1.0 copy-start.9
  7.1 0.9 copy-start.17
  8.0 49.4 %copy-start.16 = (bf16[1536,256]{1,0:T(8,128)(2,1)}, bf16[1536,256]{1,0:T(8,128)(2,1)S(1)}, u32[]{:S(2)}) copy-start(bf16[1536,256]{1,0:T(8,128)(2,1)S(1)} %bitcast_dynamic-update-slice_fusion.refs_5_) | copy-start | bytes 2359300
  366.8 90.5 %copy-start.11 = (bf16[2,256,256]{2,1,0:T(8,128)(2,1)S(1)}, bf16[2,256,256]{2,1,0:T(8,128)(2,1)}, u32[]{:S(2)}) copy-start(bf16[2,256,256]{2,1,0:T(8,128)(2,1)} %get-tuple-element.131) | copy-start | bytes 786436
  366.8 91.7 %copy-start.10 = (bf16[2,256,256]{2,1,0:T(8,128)(2,1)S(1)}, bf16[2,256,256]{2,1,0:T(8,128)(2,1)}, u32[]{:S(2)}) copy-start(bf16[2,256,256]{2,1,0:T(8,128)(2,1)} %get-tuple-element.127) | copy-start | bytes 786436
  366.8 92.7 %copy-start.8 = (bf16[2,128,896]{2,1,0:T(8,128)(2,1)S(1)}, bf16[2,128,896]{2,1,0:T(8,128)(2,1)}, u32[]{:S(2)}) copy-start(bf16[2,128,896]{2,1,0:T(8,128)(2,1)} %get-tuple-element.125) | copy-start | bytes 1376260
  457.3 3.4 copy-start.13
  457.3 3.4 copy-start.14
  457.3 3.4 copy-start.3
  457.3 3.4 copy-start.5
  459.5 2.3 copy-start.6
  459.5 2.3 copy-start.7
  469.6 1.6 copy-start.4
  469.6 2.5 copy-start.1

commit v4 on v3

--- a/solution.py
+++ b/solution.py
@@ -1865,7 +1865,7 @@
     first.add(got)
 
     hauls = [
-        Haul(0, dp, [from_input(lambda r: r.gu_sums)], [gu_spec], {BEGIN: 1, 4: 1}, swap=False),
+        Haul(0, dp, [from_input(lambda r: r.gu_sums)], [gu_spec], {BEGIN: 1, 6: 1}, swap=False),
         Haul(
             0, dp, [from_input(take_down)], [down_spec], {BEGIN: 1, 1: 1, 2: 2, 3: 1, SENT: 1}
         ),
@@ -1874,7 +1874,7 @@
             0, dp, [from_kernel(take_cat)], [cat_spec],
             {4: 1, 6: 1, SENT: 1, CHUNK: 1, CHUNK + 1: 1},
         ),
-        Straight(0, dp, from_kernel(take_shared), shared_spec, {EXTRA: 1}),
+        Haul(0, dp, [from_kernel(take_shared)], [shared_spec], {EXTRA: 1, CHUNK + 2: 2, CHUNK + 3: 2}),
     ]
     x_grads = Place(
         lambda r: (r.x_grad, r.raw.x_grad1), (rows, depth), 0,

time: 480 us -> 479 us (level)
  the two profiles are of different devices: /device:TPU:8 before, /device:TPU:0 now
where the time goes in v4:
time: 479 us; the launch traced here: 471 us
  Pallas kernels  448 us (94%)
  local copies, waits for them, and re-layouts  13.6 us (3%)
  other arithmetic  8.27 us (2%)
    pallas_call x8, Pallas kernels, exchange(): pl.pallas_call(functools.partial(exchange_kernel, plan), out_shape=shapes...  448 us

profile of v4, /device:TPU:0, one launch (start us, length us, event | category | flops | bytes accessed | tf_op | source)
XLA Modules:
  0.0 471.1 jit_solution(1186901261376481440)
XLA Ops:
  0.7 0.7 convert_element_type.24
  1.4 0.7 convert_element_type.25
  2.1 0.7 dynamic-slice_bitcast_fusion.1
  2.8 0.7 select_maximum_fusion.1
  3.5 0.6 fusion.7.refs_2_
  4.1 0.8 slice_bitcast_fusion.8
  5.0 1.9 fusion.10
  7.1 0.7 fusion.9
  8.0 52.7 %first.1 = (bf16[1024,1024]{1,0:T(8,128)(2,1)}, bf16[1024,1024]{1,0:T(8,128)(2,1)}, f32[2,4,16,256]{3,2,1,0:T(8,128)}, bf16[4,1536,256]{2,1,0:T(8,128)(2,1)}, bf16[4,4,128,256]{3,2,1,0:T(8,128)(2,1)}) custom-call(bf16[2,256,1024]{2,1,0:T(8,128)(2,1)} %refs_13_.1, bf16[2,256,1024]{2,1,0:T(8,128)(2,1)} %refs_0_.5, f32[16,256]{1,0:T(8,128)} %fusion.7.refs_2_, ...), custom_call_target="tpu_custom_call" | custom-call | flops 20000000000 | bytes 50000000 | tf_op jit(solution)/shard_map/first/pallas_call | solution.py:1496
  60.7 54.4 %mixer0.1 = (bf16[1024,1408]{1,0:T(8,128)(2,1)}, f32[1024,128]{1,0:T(8,128)}, bf16[1024,384]{1,0:T(8,128)(2,1)}, bf16[1024,512]{1,0:T(8,128)(2,1)}, bf16[8,128,3...) custom-call(bf16[2,256,1024]{2,1,0:T(8,128)(2,1)} %refs_13_.1, ...), custom_call_target="tpu_custom_call" | custom-call | flops 20000000000 | bytes 50000000 | tf_op jit(solution)/shard_map/mixer0/pallas_call | solution.py:1496
  115.1 47.2 %turn.1 = (bf16[1024,1024]{1,0:T(8,128)(2,1)}, bf16[1024,512]{1,0:T(8,128)(2,1)}, bf16[256,1024]{1,0:T(8,128)(2,1)}, bf16[1024,1024]{1,0:T(8,128)(2,1)}, bf16[4,...) custom-call(f32[256,1024]{1,0:T(8,128)} %get-tuple-element.76.refs_0_.refs_1_, ...), custom_call_target="tpu_custom_call" | custom-call | flops 20000000000 | bytes 50000000 | tf_op jit(solution)/shard_map/turn/pallas_call | solution.py:1496
  162.4 53.9 %mixer1.1 = (bf16[1024,1408]{1,0:T(8,128)(2,1)}, f32[1024,128]{1,0:T(8,128)}, bf16[1024,384]{1,0:T(8,128)(2,1)}, bf16[1024,512]{1,0:T(8,128)(2,1)}, bf16[8,128,3...) custom-call(bf16[256,1024]{1,0:T(8,128)(2,1)} %get-tuple-element.81., ...), custom_call_target="tpu_custom_call" | custom-call | flops 20000000000 | bytes 50000000 | tf_op jit(solution)/shard_map/mixer1/pallas_call | solution.py:1496
  216.3 34.1 %ffn1.1 = (f32[8,1024]{1,0:T(8,128)}, bf16[2,4,128,1024]{3,2,1,0:T(8,128)(2,1)}, bf16[2,4,256,256]{3,2,1,0:T(8,128)(2,1)}, f32[256,1024]{1,0:T(8,128)}, bf16[102...) custom-call(bf16[2,256,1024]{2,1,0:T(8,128)(2,1)} %refs_0_.5, f32[256,1024]{1,0:T(8,128)} %get-tuple-element.83.refs_1_.refs_17_, ...), custom_call_target="tpu_custom_call" | custom-call | flops 20000000000 | bytes 50000000 | tf_op jit(solution)/shard_map/ffn1/pallas_call | solution.py:1496
  250.5 75.0 %back1.1 = (bf16[256,1024]{1,0:T(8,128)(2,1)}, bf16[2,4,32,640]{3,2,1,0:T(8,128)(2,1)}, bf16[256,1024]{1,0:T(8,128)(2,1)}, bf16[1024,1024]{1,0:T(8,128)(2,1)}, b...) custom-call(f32[2,4,16,256]{3,2,1,0:T(8,128)} %get-tuple-element.72., ...), custom_call_target="tpu_custom_call" | custom-call | flops 20000000000 | bytes 50000000 | tf_op jit(solution)/shard_map/back1/pallas_call | solution.py:1496
  325.4 43.0 %ffn0.1 = (f32[8,1024]{1,0:T(8,128)}, bf16[2,4,256,256]{3,2,1,0:T(8,128)(2,1)}, f32[256,1024]{1,0:T(8,128)}, bf16[1024,1024]{1,0:T(8,128)(2,1)}, bf16[2,128,896]...) custom-call(bf16[256,1024]{1,0:T(8,128)(2,1)} %get-tuple-element.101.refs_0_.refs_14_, ...), custom_call_target="tpu_custom_call" | custom-call | flops 20000000000 | bytes 50000000 | tf_op jit(solution)/shard_map/ffn0/pallas_call | solution.py:1496
  368.4 87.3 %back0.1 = (bf16[2,128,1024]{2,1,0:T(8,128)(2,1)}, bf16[2,256,256]{2,1,0:T(8,128)(2,1)}, bf16[2,256,256]{2,1,0:T(8,128)(2,1)}, bf16[2,128,896]{2,1,0:T(8,128)(2,...) custom-call(f32[2,4,16,256]{3,2,1,0:T(8,128)} %get-tuple-element.72.refs_1_.refs_2_.re, ...), custom_call_target="tpu_custom_call" | custom-call | flops 20000000000 | bytes 50000000 | tf_op jit(solution)/shard_map/back0/pallas_call | solution.py:1496
  455.8 1.1 broadcast_select_fusion.1
  456.9 1.0 broadcast_select_fusion.2
  458.0 1.2 broadcast_select_fusion
  459.2 1.1 select_bitcast_fusion
  460.4 1.9 reshape.60
  462.3 0.6 copy.45
  462.9 0.7 copy.52
  463.6 0.7 slice_bitcast_fusion.4
  464.3 0.6 copy.42
  465.0 0.7 slice_bitcast_fusion.3
  465.7 0.8 slice_bitcast_fusion
  466.4 0.8 bitcast_convert_fusion.1
  467.3 0.1 bitcast_convert_fusion
  467.4 0.7 slice_bitcast_fusion.5
  468.2 1.5 copy.44
  469.6 1.0 copy.78
  (61 shorter events, 0.8 us)
Async XLA Ops:
  0.6 3.5 copy-start
  4.1 2.9 copy-start.12
  5.0 2.1 copy-start.15
  5.0 2.1 copy-start.2
  7.0 1.0 copy-start.9
  7.1 0.9 copy-start.17
  8.0 52.7 %copy-start.16 = (bf16[1536,256]{1,0:T(8,128)(2,1)}, bf16[1536,256]{1,0:T(8,128)(2,1)S(1)}, u32[]{:S(2)}) copy-start(bf16[1536,256]{1,0:T(8,128)(2,1)S(1)} %bitcast_dynamic-update-slice_fusion.refs_5_) | copy-start | bytes 2359300
  368.4 87.4 %copy-start.11 = (bf16[2,256,256]{2,1,0:T(8,128)(2,1)S(1)}, bf16[2,256,256]{2,1,0:T(8,128)(2,1)}, u32[]{:S(2)}) copy-start(bf16[2,256,256]{2,1,0:T(8,128)(2,1)} %get-tuple-element.131) | copy-start | bytes 786436
  368.4 88.5 %copy-start.10 = (bf16[2,256,256]{2,1,0:T(8,128)(2,1)S(1)}, bf16[2,256,256]{2,1,0:T(8,128)(2,1)}, u32[]{:S(2)}) copy-start(bf16[2,256,256]{2,1,0:T(8,128)(2,1)} %get-tuple-element.127) | copy-start | bytes 786436
  368.4 89.5 %copy-start.8 = (bf16[2,128,896]{2,1,0:T(8,128)(2,1)S(1)}, bf16[2,128,896]{2,1,0:T(8,128)(2,1)}, u32[]{:S(2)}) copy-start(bf16[2,128,896]{2,1,0:T(8,128)(2,1)} %get-tuple-element.125) | copy-start | bytes 1376260
  455.7 3.4 copy-start.13
  455.8 3.4 copy-start.14
  455.8 3.4 copy-start.3
  455.8 3.4 copy-start.5
  457.9 2.3 copy-start.6
  458.0 2.3 copy-start.7
  468.0 1.6 copy-start.4
  468.1 2.5 copy-start.1
